TPU v7x, 512 devices: a whole 4x4x16 slice. The times are simulated.
512 devices in a mesh: replica: 16 (over x_lo, y, core), section: 16 (over z), tensor: 2 (over x_hi).
Axes of the slice: x: 4 (x_hi: 2, x_lo: 2; x = x_hi * 2 + x_lo), y: 4, z: 16, core: 2. Of those that a mesh axis runs over, the one named last changes fastest.
Arguments:
- cotangent: bfloat16 [16, 3, 64, 8192], P('replica', None, None, 'tensor'), may hold values from -4 to 4
- saved_pre: bfloat16 [16, 16, 3, 64, 64], P('replica', 'section'), may hold values from -6 to 6
- up_band: bfloat16 [16, 1024, 8192], P('replica', 'section', 'tensor'), may hold values from -0.75 to 0.75
- down_band: bfloat16 [16, 1024, 8192], P('replica', 'section', 'tensor'), may hold values from -0.03125 to 0.03125
- accumulated: float32 [16, 1024, 8192], P('replica', 'section', 'tensor'), may hold values from -8 to 8
- outer_momentum: float32 [16, 2, 64, 4096], P('section', 'tensor', None, 'replica'), may hold values from -0.6 to 0.6
- band_freqs: int32 [2, 8], replicated, may hold values from 0 to 15, as said below
- sync_flags: int32 [16], P('section'), may hold values from 0 to 1, as said below
Outputs:
- residual: float32 [16, 1024, 8192], P('replica', 'section', 'tensor')
- new_outer_momentum: float32 [16, 2, 64, 4096], P('section', 'tensor', None, 'replica')
- outer_step: float32 [16, 2, 64, 4096], P('section', 'tensor', None, 'replica')
Inputs may be any that keep to these rules, and one draw needn't show every extreme that they name: `band_freqs`: each row holds 8 distinct frequencies, among them 0 and 15. `sync_flags`: exactly half of the sections have 1, the others 0.
All inputs are finite; a program needn't handle non-finite values.
Results may differ from a plain program's by a relative error of at most 0.019.
Values may be sent and summed in bfloat16 or wider, within the bound.
A program may use at most 64 MiB of HBM per device.

v0:
```python
import jax
import jax.numpy as jnp
from jax import lax
from jax.sharding import PartitionSpec as P

SPAN = 64


momentum_decay = 0.9
outer_rate = 0.7


def passed_along(block, axis, distance):
    devices = range(lax.axis_size(axis))
    route = [(i - distance, i) for i in devices if i - distance in devices]
    return lax.ppermute(block, axis, route)


def silu_slope(values):
    sigma = jax.nn.sigmoid(values)
    return sigma * (1.0 + values * (1.0 - sigma))


def dct_rows(frequencies, length):
    positions = jnp.arange(length, dtype=jnp.float32) + 0.5
    angles = jnp.pi * frequencies.astype(jnp.float32)[:, None] * positions[None, :] / length
    weights = jnp.where(frequencies[:, None] == 0, jnp.sqrt(1.0 / length), jnp.sqrt(2.0 / length))
    return weights * jnp.cos(angles)


def run_backward(grad_pieces, pre_pieces, w_down, w_up):
    section_count = lax.axis_size("section")
    position = lax.axis_index("section")
    piece_count = grad_pieces.shape[0]
    piece_rows = grad_pieces.shape[1]
    feature_count = grad_pieces.shape[2]
    band_rows = w_down.shape[0]

    def relay_tick(tick_idx, carried):
        incoming, grad_sum = carried
        piece_idx = tick_idx - (section_count - 1 - position)
        is_live = jnp.logical_and(piece_idx >= 0, piece_idx < piece_count)
        clipped = jnp.clip(piece_idx, 0, piece_count - 1)
        entering = lax.dynamic_index_in_dim(grad_pieces, clipped, 0, keepdims=False)
        grad_out = jnp.where(position == section_count - 1, entering, incoming)
        pre_now = lax.dynamic_index_in_dim(pre_pieces, clipped, 0, keepdims=False).astype(
            jnp.float32
        )
        partial_hidden = lax.dot_general(
            grad_out, w_down, (((1,), (1,)), ((), ())), preferred_element_type=jnp.float32
        )
        hidden_grad = lax.psum(partial_hidden, "tensor")
        pre_grad = (hidden_grad * silu_slope(pre_now)).astype(jnp.bfloat16)
        passed = (
            grad_out.astype(jnp.float32)
            + jnp.dot(pre_grad, w_up, preferred_element_type=jnp.float32)
        ).astype(jnp.bfloat16)
        hidden = jax.nn.silu(pre_now).astype(jnp.bfloat16)
        contrib = lax.dot_general(
            hidden, grad_out, (((0,), (0,)), ((), ())), preferred_element_type=jnp.float32
        )
        grad_sum = grad_sum + jnp.where(is_live, contrib, 0.0)
        incoming = passed_along(passed, "section", -1)
        return (incoming, grad_sum)

    initial = (
        jnp.zeros((piece_rows, feature_count), jnp.bfloat16),
        jnp.zeros((band_rows, feature_count), jnp.float32),
    )
    finished = lax.fori_loop(0, section_count + piece_count - 1, relay_tick, initial)
    return finished[1]


def local(
    cotangent, saved_pre, up_band, down_band, accumulated, outer_momentum, band_freqs, sync_flags
):
    highest = lax.Precision.HIGHEST
    feature_count = cotangent.shape[3]
    band_rows = down_band.shape[1]
    grad_pieces = cotangent[0]
    pre_pieces = saved_pre[0, 0]
    grad_sum = run_backward(grad_pieces, pre_pieces, down_band[0], up_band[0])
    moment = accumulated[0] + grad_sum
    row_basis = dct_rows(band_freqs[0], SPAN)
    col_basis = dct_rows(band_freqs[1], SPAN)
    groups = band_rows // SPAN
    blocks = feature_count // SPAN
    tile_view = moment.reshape(groups, SPAN, blocks, SPAN)
    coeffs = jnp.einsum("ui,gicj->gucj", row_basis, tile_view, precision=highest)
    coeffs = jnp.einsum("gucj,vj->gucv", coeffs, col_basis, precision=highest)
    totals = lax.psum_scatter(coeffs, "replica", scatter_dimension=2, tiled=True)
    half_back = jnp.einsum("gucv,vj->gucj", coeffs, col_basis, precision=highest)
    decoded = jnp.einsum("ui,gucj->gicj", row_basis, half_back, precision=highest).reshape(
        band_rows, feature_count
    )
    synced = sync_flags[0] == 1
    residual = jnp.where(synced, moment - decoded, moment)
    mean_coeffs = totals / lax.axis_size("replica")
    half_back = jnp.einsum("gucv,vj->gucj", mean_coeffs, col_basis, precision=highest)
    change = jnp.einsum("ui,gucj->gicj", row_basis, half_back, precision=highest).reshape(
        band_rows, -1
    )
    prior = outer_momentum[0, 0]
    new_moment = momentum_decay * prior + change
    stepped = -outer_rate * (change + momentum_decay * new_moment)
    new_outer = jnp.where(synced, new_moment, prior)
    outer_step = jnp.where(synced, stepped, jnp.zeros_like(stepped))
    return (residual[None], new_outer[None, None], outer_step[None, None])


def solution(mesh):
    return jax.shard_map(
        local,
        mesh=mesh,
        in_specs=(
            P("replica", None, None, "tensor"),
            P("replica", "section", None, None, None),
            P("replica", "section", "tensor"),
            P("replica", "section", "tensor"),
            P("replica", "section", "tensor"),
            P("section", "tensor", None, "replica"),
            P(),
            P("section"),
        ),
        out_specs=(
            P("replica", "section", "tensor"),
            P("section", "tensor", None, "replica"),
            P("section", "tensor", None, "replica"),
        ),
        check_vma=False,
    )
```

profile of v0, /device:TPU:1, one launch (start us, length us, event | category | flops | bytes accessed | tf_op | source)
XLA Modules:
  0.0 573.4 jit_solution(11793796626256761957)
XLA Ops:
  8.0 421.0 %while.18 = (s32[]{:T(128)}, bf16[64,4096]{1,0:T(8,128)(2,1)S(1)}, f32[64,4096]{1,0:T(8,128)S(1)}, pred[]{:T(512)}, s32[]{:T(128)}, /*index=5*/bf16[3,64,4096]{2...) while((s32[]{:T(128)}, bf16[64,4096]{1,0:T(8,128)(2,1)S(1)}, ...), condition=%wide.region_2.3_spmd.clone, body=%wide.region_0.2_spmd.clone.sunk | while | flops 102567936 | bytes 11223342 | solution.py:70
  9.2 1.3 fusion.100
  10.6 10.2 %psum.15 = f32[64,64]{1,0:T(8,128)S(1)} all-reduce(f32[64,64]{1,0:T(8,128)S(1)} %fusion.100), channel_id=1, replica_groups=mesh['replica'=16,'section'=16,'tensor'=2] {'tensor'}, use_global_device_ids=true, to_apply=%region_1.1 | all-reduce | flops 4096 | bytes 32768 | tf_op jit(solution)/shard_map/while/body/eval_jaxpr/psum | solution.py:52
  22.8 8.9 %collective-permute-done = bf16[64,4096]{1,0:T(8,128)(2,1)S(1)} collective-permute-done((bf16[64,4096]{1,0:T(8,128)(2,1)S(1)}, bf16[64,4096]{1,0:T(8,128)(2,1)S(1)}, u32[]{:S(2)}, u32[]{:S(2)}) %collective-permute-start) | collective-permute-done | bytes 524320 | tf_op jit(solution)/shard_map/while/body/eval_jaxpr/ppermute | solution.py:16
  32.9 1.3 fusion.100
  34.2 6.7 %psum.15 = f32[64,64]{1,0:T(8,128)S(1)} all-reduce(f32[64,64]{1,0:T(8,128)S(1)} %fusion.100), channel_id=1, replica_groups=mesh['replica'=16,'section'=16,'tensor'=2] {'tensor'}, use_global_device_ids=true, to_apply=%region_1.1 | all-reduce | flops 4096 | bytes 32768 | tf_op jit(solution)/shard_map/while/body/eval_jaxpr/psum | solution.py:52
  42.9 11.1 %collective-permute-done = bf16[64,4096]{1,0:T(8,128)(2,1)S(1)} collective-permute-done((bf16[64,4096]{1,0:T(8,128)(2,1)S(1)}, bf16[64,4096]{1,0:T(8,128)(2,1)S(1)}, u32[]{:S(2)}, u32[]{:S(2)}) %collective-permute-start) | collective-permute-done | bytes 524320 | tf_op jit(solution)/shard_map/while/body/eval_jaxpr/ppermute | solution.py:16
  55.2 1.3 fusion.100
  56.6 9.2 %psum.15 = f32[64,64]{1,0:T(8,128)S(1)} all-reduce(f32[64,64]{1,0:T(8,128)S(1)} %fusion.100), channel_id=1, replica_groups=mesh['replica'=16,'section'=16,'tensor'=2] {'tensor'}, use_global_device_ids=true, to_apply=%region_1.1 | all-reduce | flops 4096 | bytes 32768 | tf_op jit(solution)/shard_map/while/body/eval_jaxpr/psum | solution.py:52
  67.8 9.2 %collective-permute-done = bf16[64,4096]{1,0:T(8,128)(2,1)S(1)} collective-permute-done((bf16[64,4096]{1,0:T(8,128)(2,1)S(1)}, bf16[64,4096]{1,0:T(8,128)(2,1)S(1)}, u32[]{:S(2)}, u32[]{:S(2)}) %collective-permute-start) | collective-permute-done | bytes 524320 | tf_op jit(solution)/shard_map/while/body/eval_jaxpr/ppermute | solution.py:16
  78.2 1.3 fusion.100
  79.5 6.7 %psum.15 = f32[64,64]{1,0:T(8,128)S(1)} all-reduce(f32[64,64]{1,0:T(8,128)S(1)} %fusion.100), channel_id=1, replica_groups=mesh['replica'=16,'section'=16,'tensor'=2] {'tensor'}, use_global_device_ids=true, to_apply=%region_1.1 | all-reduce | flops 4096 | bytes 32768 | tf_op jit(solution)/shard_map/while/body/eval_jaxpr/psum | solution.py:52
  88.3 9.9 %collective-permute-done = bf16[64,4096]{1,0:T(8,128)(2,1)S(1)} collective-permute-done((bf16[64,4096]{1,0:T(8,128)(2,1)S(1)}, bf16[64,4096]{1,0:T(8,128)(2,1)S(1)}, u32[]{:S(2)}, u32[]{:S(2)}) %collective-permute-start) | collective-permute-done | bytes 524320 | tf_op jit(solution)/shard_map/while/body/eval_jaxpr/ppermute | solution.py:16
  99.4 1.3 fusion.100
  100.7 9.2 %psum.15 = f32[64,64]{1,0:T(8,128)S(1)} all-reduce(f32[64,64]{1,0:T(8,128)S(1)} %fusion.100), channel_id=1, replica_groups=mesh['replica'=16,'section'=16,'tensor'=2] {'tensor'}, use_global_device_ids=true, to_apply=%region_1.1 | all-reduce | flops 4096 | bytes 32768 | tf_op jit(solution)/shard_map/while/body/eval_jaxpr/psum | solution.py:52
  112.1 8.8 %collective-permute-done = bf16[64,4096]{1,0:T(8,128)(2,1)S(1)} collective-permute-done((bf16[64,4096]{1,0:T(8,128)(2,1)S(1)}, bf16[64,4096]{1,0:T(8,128)(2,1)S(1)}, u32[]{:S(2)}, u32[]{:S(2)}) %collective-permute-start) | collective-permute-done | bytes 524320 | tf_op jit(solution)/shard_map/while/body/eval_jaxpr/ppermute | solution.py:16
  122.1 1.3 fusion.100
  123.4 6.8 %psum.15 = f32[64,64]{1,0:T(8,128)S(1)} all-reduce(f32[64,64]{1,0:T(8,128)S(1)} %fusion.100), channel_id=1, replica_groups=mesh['replica'=16,'section'=16,'tensor'=2] {'tensor'}, use_global_device_ids=true, to_apply=%region_1.1 | all-reduce | flops 4096 | bytes 32768 | tf_op jit(solution)/shard_map/while/body/eval_jaxpr/psum | solution.py:52
  132.3 9.5 %collective-permute-done = bf16[64,4096]{1,0:T(8,128)(2,1)S(1)} collective-permute-done((bf16[64,4096]{1,0:T(8,128)(2,1)S(1)}, bf16[64,4096]{1,0:T(8,128)(2,1)S(1)}, u32[]{:S(2)}, u32[]{:S(2)}) %collective-permute-start) | collective-permute-done | bytes 524320 | tf_op jit(solution)/shard_map/while/body/eval_jaxpr/ppermute | solution.py:16
  143.0 1.3 fusion.100
  144.3 9.3 %psum.15 = f32[64,64]{1,0:T(8,128)S(1)} all-reduce(f32[64,64]{1,0:T(8,128)S(1)} %fusion.100), channel_id=1, replica_groups=mesh['replica'=16,'section'=16,'tensor'=2] {'tensor'}, use_global_device_ids=true, to_apply=%region_1.1 | all-reduce | flops 4096 | bytes 32768 | tf_op jit(solution)/shard_map/while/body/eval_jaxpr/psum | solution.py:52
  155.7 10.0 %collective-permute-done = bf16[64,4096]{1,0:T(8,128)(2,1)S(1)} collective-permute-done((bf16[64,4096]{1,0:T(8,128)(2,1)S(1)}, bf16[64,4096]{1,0:T(8,128)(2,1)S(1)}, u32[]{:S(2)}, u32[]{:S(2)}) %collective-permute-start) | collective-permute-done | bytes 524320 | tf_op jit(solution)/shard_map/while/body/eval_jaxpr/ppermute | solution.py:16
  166.8 1.3 fusion.100
  168.1 8.5 %psum.15 = f32[64,64]{1,0:T(8,128)S(1)} all-reduce(f32[64,64]{1,0:T(8,128)S(1)} %fusion.100), channel_id=1, replica_groups=mesh['replica'=16,'section'=16,'tensor'=2] {'tensor'}, use_global_device_ids=true, to_apply=%region_1.1 | all-reduce | flops 4096 | bytes 32768 | tf_op jit(solution)/shard_map/while/body/eval_jaxpr/psum | solution.py:52
  178.7 14.3 %collective-permute-done = bf16[64,4096]{1,0:T(8,128)(2,1)S(1)} collective-permute-done((bf16[64,4096]{1,0:T(8,128)(2,1)S(1)}, bf16[64,4096]{1,0:T(8,128)(2,1)S(1)}, u32[]{:S(2)}, u32[]{:S(2)}) %collective-permute-start) | collective-permute-done | bytes 524320 | tf_op jit(solution)/shard_map/while/body/eval_jaxpr/ppermute | solution.py:16
  194.2 1.3 fusion.100
  195.5 6.9 %psum.15 = f32[64,64]{1,0:T(8,128)S(1)} all-reduce(f32[64,64]{1,0:T(8,128)S(1)} %fusion.100), channel_id=1, replica_groups=mesh['replica'=16,'section'=16,'tensor'=2] {'tensor'}, use_global_device_ids=true, to_apply=%region_1.1 | all-reduce | flops 4096 | bytes 32768 | tf_op jit(solution)/shard_map/while/body/eval_jaxpr/psum | solution.py:52
  202.7 1.3 collective-permute-start
  204.4 13.7 %collective-permute-done = bf16[64,4096]{1,0:T(8,128)(2,1)S(1)} collective-permute-done((bf16[64,4096]{1,0:T(8,128)(2,1)S(1)}, bf16[64,4096]{1,0:T(8,128)(2,1)S(1)}, u32[]{:S(2)}, u32[]{:S(2)}) %collective-permute-start) | collective-permute-done | bytes 524320 | tf_op jit(solution)/shard_map/while/body/eval_jaxpr/ppermute | solution.py:16
  219.3 1.3 fusion.100
  220.6 9.3 %psum.15 = f32[64,64]{1,0:T(8,128)S(1)} all-reduce(f32[64,64]{1,0:T(8,128)S(1)} %fusion.100), channel_id=1, replica_groups=mesh['replica'=16,'section'=16,'tensor'=2] {'tensor'}, use_global_device_ids=true, to_apply=%region_1.1 | all-reduce | flops 4096 | bytes 32768 | tf_op jit(solution)/shard_map/while/body/eval_jaxpr/psum | solution.py:52
  230.2 1.3 collective-permute-start
  231.9 10.5 %collective-permute-done = bf16[64,4096]{1,0:T(8,128)(2,1)S(1)} collective-permute-done((bf16[64,4096]{1,0:T(8,128)(2,1)S(1)}, bf16[64,4096]{1,0:T(8,128)(2,1)S(1)}, u32[]{:S(2)}, u32[]{:S(2)}) %collective-permute-start) | collective-permute-done | bytes 524320 | tf_op jit(solution)/shard_map/while/body/eval_jaxpr/ppermute | solution.py:16
  243.6 1.3 fusion.100
  244.9 7.2 %psum.15 = f32[64,64]{1,0:T(8,128)S(1)} all-reduce(f32[64,64]{1,0:T(8,128)S(1)} %fusion.100), channel_id=1, replica_groups=mesh['replica'=16,'section'=16,'tensor'=2] {'tensor'}, use_global_device_ids=true, to_apply=%region_1.1 | all-reduce | flops 4096 | bytes 32768 | tf_op jit(solution)/shard_map/while/body/eval_jaxpr/psum | solution.py:52
  252.4 1.3 collective-permute-start
  254.2 9.8 %collective-permute-done = bf16[64,4096]{1,0:T(8,128)(2,1)S(1)} collective-permute-done((bf16[64,4096]{1,0:T(8,128)(2,1)S(1)}, bf16[64,4096]{1,0:T(8,128)(2,1)S(1)}, u32[]{:S(2)}, u32[]{:S(2)}) %collective-permute-start) | collective-permute-done | bytes 524320 | tf_op jit(solution)/shard_map/while/body/eval_jaxpr/ppermute | solution.py:16
  265.2 1.3 fusion.100
  266.5 9.0 %psum.15 = f32[64,64]{1,0:T(8,128)S(1)} all-reduce(f32[64,64]{1,0:T(8,128)S(1)} %fusion.100), channel_id=1, replica_groups=mesh['replica'=16,'section'=16,'tensor'=2] {'tensor'}, use_global_device_ids=true, to_apply=%region_1.1 | all-reduce | flops 4096 | bytes 32768 | tf_op jit(solution)/shard_map/while/body/eval_jaxpr/psum | solution.py:52
  277.6 8.9 %collective-permute-done = bf16[64,4096]{1,0:T(8,128)(2,1)S(1)} collective-permute-done((bf16[64,4096]{1,0:T(8,128)(2,1)S(1)}, bf16[64,4096]{1,0:T(8,128)(2,1)S(1)}, u32[]{:S(2)}, u32[]{:S(2)}) %collective-permute-start) | collective-permute-done | bytes 524320 | tf_op jit(solution)/shard_map/while/body/eval_jaxpr/ppermute | solution.py:16
  287.7 1.3 fusion.100
  289.0 7.1 %psum.15 = f32[64,64]{1,0:T(8,128)S(1)} all-reduce(f32[64,64]{1,0:T(8,128)S(1)} %fusion.100), channel_id=1, replica_groups=mesh['replica'=16,'section'=16,'tensor'=2] {'tensor'}, use_global_device_ids=true, to_apply=%region_1.1 | all-reduce | flops 4096 | bytes 32768 | tf_op jit(solution)/shard_map/while/body/eval_jaxpr/psum | solution.py:52
  298.2 9.1 %collective-permute-done = bf16[64,4096]{1,0:T(8,128)(2,1)S(1)} collective-permute-done((bf16[64,4096]{1,0:T(8,128)(2,1)S(1)}, bf16[64,4096]{1,0:T(8,128)(2,1)S(1)}, u32[]{:S(2)}, u32[]{:S(2)}) %collective-permute-start) | collective-permute-done | bytes 524320 | tf_op jit(solution)/shard_map/while/body/eval_jaxpr/ppermute | solution.py:16
  308.5 1.3 fusion.100
  309.8 9.0 %psum.15 = f32[64,64]{1,0:T(8,128)S(1)} all-reduce(f32[64,64]{1,0:T(8,128)S(1)} %fusion.100), channel_id=1, replica_groups=mesh['replica'=16,'section'=16,'tensor'=2] {'tensor'}, use_global_device_ids=true, to_apply=%region_1.1 | all-reduce | flops 4096 | bytes 32768 | tf_op jit(solution)/shard_map/while/body/eval_jaxpr/psum | solution.py:52
  320.9 9.8 %collective-permute-done = bf16[64,4096]{1,0:T(8,128)(2,1)S(1)} collective-permute-done((bf16[64,4096]{1,0:T(8,128)(2,1)S(1)}, bf16[64,4096]{1,0:T(8,128)(2,1)S(1)}, u32[]{:S(2)}, u32[]{:S(2)}) %collective-permute-start) | collective-permute-done | bytes 524320 | tf_op jit(solution)/shard_map/while/body/eval_jaxpr/ppermute | solution.py:16
  331.9 1.3 fusion.100
  333.2 6.8 %psum.15 = f32[64,64]{1,0:T(8,128)S(1)} all-reduce(f32[64,64]{1,0:T(8,128)S(1)} %fusion.100), channel_id=1, replica_groups=mesh['replica'=16,'section'=16,'tensor'=2] {'tensor'}, use_global_device_ids=true, to_apply=%region_1.1 | all-reduce | flops 4096 | bytes 32768 | tf_op jit(solution)/shard_map/while/body/eval_jaxpr/psum | solution.py:52
  342.1 11.4 %collective-permute-done = bf16[64,4096]{1,0:T(8,128)(2,1)S(1)} collective-permute-done((bf16[64,4096]{1,0:T(8,128)(2,1)S(1)}, bf16[64,4096]{1,0:T(8,128)(2,1)S(1)}, u32[]{:S(2)}, u32[]{:S(2)}) %collective-permute-start) | collective-permute-done | bytes 524320 | tf_op jit(solution)/shard_map/while/body/eval_jaxpr/ppermute | solution.py:16
  354.7 1.3 fusion.100
  356.0 7.7 %psum.15 = f32[64,64]{1,0:T(8,128)S(1)} all-reduce(f32[64,64]{1,0:T(8,128)S(1)} %fusion.100), channel_id=1, replica_groups=mesh['replica'=16,'section'=16,'tensor'=2] {'tensor'}, use_global_device_ids=true, to_apply=%region_1.1 | all-reduce | flops 4096 | bytes 32768 | tf_op jit(solution)/shard_map/while/body/eval_jaxpr/psum | solution.py:52
  365.8 12.9 %collective-permute-done = bf16[64,4096]{1,0:T(8,128)(2,1)S(1)} collective-permute-done((bf16[64,4096]{1,0:T(8,128)(2,1)S(1)}, bf16[64,4096]{1,0:T(8,128)(2,1)S(1)}, u32[]{:S(2)}, u32[]{:S(2)}) %collective-permute-start) | collective-permute-done | bytes 524320 | tf_op jit(solution)/shard_map/while/body/eval_jaxpr/ppermute | solution.py:16
  379.8 1.3 fusion.100
  381.2 10.3 %psum.15 = f32[64,64]{1,0:T(8,128)S(1)} all-reduce(f32[64,64]{1,0:T(8,128)S(1)} %fusion.100), channel_id=1, replica_groups=mesh['replica'=16,'section'=16,'tensor'=2] {'tensor'}, use_global_device_ids=true, to_apply=%region_1.1 | all-reduce | flops 4096 | bytes 32768 | tf_op jit(solution)/shard_map/while/body/eval_jaxpr/psum | solution.py:52
  393.5 13.3 %collective-permute-done = bf16[64,4096]{1,0:T(8,128)(2,1)S(1)} collective-permute-done((bf16[64,4096]{1,0:T(8,128)(2,1)S(1)}, bf16[64,4096]{1,0:T(8,128)(2,1)S(1)}, u32[]{:S(2)}, u32[]{:S(2)}) %collective-permute-start) | collective-permute-done | bytes 524320 | tf_op jit(solution)/shard_map/while/body/eval_jaxpr/ppermute | solution.py:16
  407.9 1.3 fusion.100
  409.3 7.7 %psum.15 = f32[64,64]{1,0:T(8,128)S(1)} all-reduce(f32[64,64]{1,0:T(8,128)S(1)} %fusion.100), channel_id=1, replica_groups=mesh['replica'=16,'section'=16,'tensor'=2] {'tensor'}, use_global_device_ids=true, to_apply=%region_1.1 | all-reduce | flops 4096 | bytes 32768 | tf_op jit(solution)/shard_map/while/body/eval_jaxpr/psum | solution.py:52
  419.0 10.0 %collective-permute-done = bf16[64,4096]{1,0:T(8,128)(2,1)S(1)} collective-permute-done((bf16[64,4096]{1,0:T(8,128)(2,1)S(1)}, bf16[64,4096]{1,0:T(8,128)(2,1)S(1)}, u32[]{:S(2)}, u32[]{:S(2)}) %collective-permute-start) | collective-permute-done | bytes 524320 | tf_op jit(solution)/shard_map/while/body/eval_jaxpr/ppermute | solution.py:16
  429.0 1.3 bitcast_add_fusion
  430.4 2.2 reshape.93
  432.5 3.9 fusion.24
  438.7 4.8 fusion.28
  443.5 2.2 copy.18
  447.4 116.9 %reduce-scatter.2.cloned.1.call-done = f32[1,8,4,8]{3,1,0,2:T(8,128)} async-done(((f32[1,8,64,8]{3,1,0,2:T(8,128)}), f32[1,8,4,8]{3,1,0,2:T(8,128)}) %reduce-scatter.2.cloned.1.call-update) | async-done | bytes 1040 | tf_op jit(solution)/shard_map/reduce_scatter | solution.py:91
  (157 shorter events, 59.5 us)
Async XLA Ops:
  7.2 557.2 %reduce-scatter.2.cloned.1.call-start = ((), (), s32[]{:S(2)}) async-start(), calls=%async_computation.1 | async-start | bytes 278528 | tf_op jit(solution)/shard_map/reduce_scatter | solution.py:91
  8.1 12.7 %copy-start = (bf16[64,4096]{1,0:T(8,128)(2,1)S(1)}, bf16[64,4096]{1,0:T(8,128)(2,1)}, u32[]{:S(2)}) copy-start(bf16[64,4096]{1,0:T(8,128)(2,1)} %get-tuple-element.343) | copy-start | bytes 1572868 | tf_op jit(solution)/shard_map/while
  8.1 12.7 %copy-start.1 = (bf16[3,64,64]{2,1,0:T(8,128)(2,1)S(1)}, bf16[3,64,64]{2,1,0:T(8,128)(2,1)}, u32[]{:S(2)}) copy-start(bf16[3,64,64]{2,1,0:T(8,128)(2,1)} %get-tuple-element.342) | copy-start | bytes 73732 | tf_op jit(solution)/shard_map/while
  21.1 10.6 %collective-permute-start = (bf16[64,4096]{1,0:T(8,128)(2,1)S(1)}, bf16[64,4096]{1,0:T(8,128)(2,1)S(1)}, u32[]{:S(2)}, u32[]{:S(2)}) collective-permute-start(bf16[64,4096]{1,0:T(8,128)(2,1)S(1)} %fusion.101), channel_id=1, source_target_pairs={{2,0},{4,2},{6,4},{8,6},{10,8},{12,10},{14,12},{16,14},{18,16},{20... | collective-permute-start | bytes 1572872 | tf_op jit(solution)/shard_map/while/body/eval_jaxpr/ppermute | solution.py:16
  31.7 9.2 %copy-start = (bf16[64,4096]{1,0:T(8,128)(2,1)S(1)}, bf16[64,4096]{1,0:T(8,128)(2,1)}, u32[]{:S(2)}) copy-start(bf16[64,4096]{1,0:T(8,128)(2,1)} %get-tuple-element.343) | copy-start | bytes 1572868 | tf_op jit(solution)/shard_map/while
  31.7 9.2 %copy-start.1 = (bf16[3,64,64]{2,1,0:T(8,128)(2,1)S(1)}, bf16[3,64,64]{2,1,0:T(8,128)(2,1)}, u32[]{:S(2)}) copy-start(bf16[3,64,64]{2,1,0:T(8,128)(2,1)} %get-tuple-element.342) | copy-start | bytes 73732 | tf_op jit(solution)/shard_map/while
  41.2 12.9 %collective-permute-start = (bf16[64,4096]{1,0:T(8,128)(2,1)S(1)}, bf16[64,4096]{1,0:T(8,128)(2,1)S(1)}, u32[]{:S(2)}, u32[]{:S(2)}) collective-permute-start(bf16[64,4096]{1,0:T(8,128)(2,1)S(1)} %fusion.101), channel_id=1, source_target_pairs={{2,0},{4,2},{6,4},{8,6},{10,8},{12,10},{14,12},{16,14},{18,16},{20... | collective-permute-start | bytes 1572872 | tf_op jit(solution)/shard_map/while/body/eval_jaxpr/ppermute | solution.py:16
  54.1 11.7 %copy-start = (bf16[64,4096]{1,0:T(8,128)(2,1)S(1)}, bf16[64,4096]{1,0:T(8,128)(2,1)}, u32[]{:S(2)}) copy-start(bf16[64,4096]{1,0:T(8,128)(2,1)} %get-tuple-element.343) | copy-start | bytes 1572868 | tf_op jit(solution)/shard_map/while
  54.1 11.7 %copy-start.1 = (bf16[3,64,64]{2,1,0:T(8,128)(2,1)S(1)}, bf16[3,64,64]{2,1,0:T(8,128)(2,1)}, u32[]{:S(2)}) copy-start(bf16[3,64,64]{2,1,0:T(8,128)(2,1)} %get-tuple-element.342) | copy-start | bytes 73732 | tf_op jit(solution)/shard_map/while
  66.1 11.0 %collective-permute-start = (bf16[64,4096]{1,0:T(8,128)(2,1)S(1)}, bf16[64,4096]{1,0:T(8,128)(2,1)S(1)}, u32[]{:S(2)}, u32[]{:S(2)}) collective-permute-start(bf16[64,4096]{1,0:T(8,128)(2,1)S(1)} %fusion.101), channel_id=1, source_target_pairs={{2,0},{4,2},{6,4},{8,6},{10,8},{12,10},{14,12},{16,14},{18,16},{20... | collective-permute-start | bytes 1572872 | tf_op jit(solution)/shard_map/while/body/eval_jaxpr/ppermute | solution.py:16
  77.1 9.2 %copy-start = (bf16[64,4096]{1,0:T(8,128)(2,1)S(1)}, bf16[64,4096]{1,0:T(8,128)(2,1)}, u32[]{:S(2)}) copy-start(bf16[64,4096]{1,0:T(8,128)(2,1)} %get-tuple-element.343) | copy-start | bytes 1572868 | tf_op jit(solution)/shard_map/while
  77.1 9.2 %copy-start.1 = (bf16[3,64,64]{2,1,0:T(8,128)(2,1)S(1)}, bf16[3,64,64]{2,1,0:T(8,128)(2,1)}, u32[]{:S(2)}) copy-start(bf16[3,64,64]{2,1,0:T(8,128)(2,1)} %get-tuple-element.342) | copy-start | bytes 73732 | tf_op jit(solution)/shard_map/while
  86.6 11.7 %collective-permute-start = (bf16[64,4096]{1,0:T(8,128)(2,1)S(1)}, bf16[64,4096]{1,0:T(8,128)(2,1)S(1)}, u32[]{:S(2)}, u32[]{:S(2)}) collective-permute-start(bf16[64,4096]{1,0:T(8,128)(2,1)S(1)} %fusion.101), channel_id=1, source_target_pairs={{2,0},{4,2},{6,4},{8,6},{10,8},{12,10},{14,12},{16,14},{18,16},{20... | collective-permute-start | bytes 1572872 | tf_op jit(solution)/shard_map/while/body/eval_jaxpr/ppermute | solution.py:16
  98.3 11.8 %copy-start = (bf16[64,4096]{1,0:T(8,128)(2,1)S(1)}, bf16[64,4096]{1,0:T(8,128)(2,1)}, u32[]{:S(2)}) copy-start(bf16[64,4096]{1,0:T(8,128)(2,1)} %get-tuple-element.343) | copy-start | bytes 1572868 | tf_op jit(solution)/shard_map/while
  98.3 11.8 %copy-start.1 = (bf16[3,64,64]{2,1,0:T(8,128)(2,1)S(1)}, bf16[3,64,64]{2,1,0:T(8,128)(2,1)}, u32[]{:S(2)}) copy-start(bf16[3,64,64]{2,1,0:T(8,128)(2,1)} %get-tuple-element.342) | copy-start | bytes 73732 | tf_op jit(solution)/shard_map/while
  110.3 10.6 %collective-permute-start = (bf16[64,4096]{1,0:T(8,128)(2,1)S(1)}, bf16[64,4096]{1,0:T(8,128)(2,1)S(1)}, u32[]{:S(2)}, u32[]{:S(2)}) collective-permute-start(bf16[64,4096]{1,0:T(8,128)(2,1)S(1)} %fusion.101), channel_id=1, source_target_pairs={{2,0},{4,2},{6,4},{8,6},{10,8},{12,10},{14,12},{16,14},{18,16},{20... | collective-permute-start | bytes 1572872 | tf_op jit(solution)/shard_map/while/body/eval_jaxpr/ppermute | solution.py:16
  120.9 9.3 %copy-start = (bf16[64,4096]{1,0:T(8,128)(2,1)S(1)}, bf16[64,4096]{1,0:T(8,128)(2,1)}, u32[]{:S(2)}) copy-start(bf16[64,4096]{1,0:T(8,128)(2,1)} %get-tuple-element.343) | copy-start | bytes 1572868 | tf_op jit(solution)/shard_map/while
  120.9 9.4 %copy-start.1 = (bf16[3,64,64]{2,1,0:T(8,128)(2,1)S(1)}, bf16[3,64,64]{2,1,0:T(8,128)(2,1)}, u32[]{:S(2)}) copy-start(bf16[3,64,64]{2,1,0:T(8,128)(2,1)} %get-tuple-element.342) | copy-start | bytes 73732 | tf_op jit(solution)/shard_map/while
  130.6 11.3 %collective-permute-start = (bf16[64,4096]{1,0:T(8,128)(2,1)S(1)}, bf16[64,4096]{1,0:T(8,128)(2,1)S(1)}, u32[]{:S(2)}, u32[]{:S(2)}) collective-permute-start(bf16[64,4096]{1,0:T(8,128)(2,1)S(1)} %fusion.101), channel_id=1, source_target_pairs={{2,0},{4,2},{6,4},{8,6},{10,8},{12,10},{14,12},{16,14},{18,16},{20... | collective-permute-start | bytes 1572872 | tf_op jit(solution)/shard_map/while/body/eval_jaxpr/ppermute | solution.py:16
  141.8 11.8 %copy-start = (bf16[64,4096]{1,0:T(8,128)(2,1)S(1)}, bf16[64,4096]{1,0:T(8,128)(2,1)}, u32[]{:S(2)}) copy-start(bf16[64,4096]{1,0:T(8,128)(2,1)} %get-tuple-element.343) | copy-start | bytes 1572868 | tf_op jit(solution)/shard_map/while
  141.8 11.8 %copy-start.1 = (bf16[3,64,64]{2,1,0:T(8,128)(2,1)S(1)}, bf16[3,64,64]{2,1,0:T(8,128)(2,1)}, u32[]{:S(2)}) copy-start(bf16[3,64,64]{2,1,0:T(8,128)(2,1)} %get-tuple-element.342) | copy-start | bytes 73732 | tf_op jit(solution)/shard_map/while
  153.9 11.7 %collective-permute-start = (bf16[64,4096]{1,0:T(8,128)(2,1)S(1)}, bf16[64,4096]{1,0:T(8,128)(2,1)S(1)}, u32[]{:S(2)}, u32[]{:S(2)}) collective-permute-start(bf16[64,4096]{1,0:T(8,128)(2,1)S(1)} %fusion.101), channel_id=1, source_target_pairs={{2,0},{4,2},{6,4},{8,6},{10,8},{12,10},{14,12},{16,14},{18,16},{20... | collective-permute-start | bytes 1572872 | tf_op jit(solution)/shard_map/while/body/eval_jaxpr/ppermute | solution.py:16
  165.6 11.0 %copy-start = (bf16[64,4096]{1,0:T(8,128)(2,1)S(1)}, bf16[64,4096]{1,0:T(8,128)(2,1)}, u32[]{:S(2)}) copy-start(bf16[64,4096]{1,0:T(8,128)(2,1)} %get-tuple-element.343) | copy-start | bytes 1572868 | tf_op jit(solution)/shard_map/while
  165.6 11.0 %copy-start.1 = (bf16[3,64,64]{2,1,0:T(8,128)(2,1)S(1)}, bf16[3,64,64]{2,1,0:T(8,128)(2,1)}, u32[]{:S(2)}) copy-start(bf16[3,64,64]{2,1,0:T(8,128)(2,1)} %get-tuple-element.342) | copy-start | bytes 73732 | tf_op jit(solution)/shard_map/while
  177.0 16.0 %collective-permute-start = (bf16[64,4096]{1,0:T(8,128)(2,1)S(1)}, bf16[64,4096]{1,0:T(8,128)(2,1)S(1)}, u32[]{:S(2)}, u32[]{:S(2)}) collective-permute-start(bf16[64,4096]{1,0:T(8,128)(2,1)S(1)} %fusion.101), channel_id=1, source_target_pairs={{2,0},{4,2},{6,4},{8,6},{10,8},{12,10},{14,12},{16,14},{18,16},{20... | collective-permute-start | bytes 1572872 | tf_op jit(solution)/shard_map/while/body/eval_jaxpr/ppermute | solution.py:16
  193.0 9.4 %copy-start = (bf16[64,4096]{1,0:T(8,128)(2,1)S(1)}, bf16[64,4096]{1,0:T(8,128)(2,1)}, u32[]{:S(2)}) copy-start(bf16[64,4096]{1,0:T(8,128)(2,1)} %get-tuple-element.343) | copy-start | bytes 1572868 | tf_op jit(solution)/shard_map/while
  193.0 9.4 %copy-start.1 = (bf16[3,64,64]{2,1,0:T(8,128)(2,1)S(1)}, bf16[3,64,64]{2,1,0:T(8,128)(2,1)}, u32[]{:S(2)}) copy-start(bf16[3,64,64]{2,1,0:T(8,128)(2,1)} %get-tuple-element.342) | copy-start | bytes 73732 | tf_op jit(solution)/shard_map/while
  202.7 15.4 %collective-permute-start = (bf16[64,4096]{1,0:T(8,128)(2,1)S(1)}, bf16[64,4096]{1,0:T(8,128)(2,1)S(1)}, u32[]{:S(2)}, u32[]{:S(2)}) collective-permute-start(bf16[64,4096]{1,0:T(8,128)(2,1)S(1)} %fusion.101), channel_id=1, source_target_pairs={{2,0},{4,2},{6,4},{8,6},{10,8},{12,10},{14,12},{16,14},{18,16},{20... | collective-permute-start | bytes 1572872 | tf_op jit(solution)/shard_map/while/body/eval_jaxpr/ppermute | solution.py:16
  218.1 11.8 %copy-start = (bf16[64,4096]{1,0:T(8,128)(2,1)S(1)}, bf16[64,4096]{1,0:T(8,128)(2,1)}, u32[]{:S(2)}) copy-start(bf16[64,4096]{1,0:T(8,128)(2,1)} %get-tuple-element.343) | copy-start | bytes 1572868 | tf_op jit(solution)/shard_map/while
  218.1 11.8 %copy-start.1 = (bf16[3,64,64]{2,1,0:T(8,128)(2,1)S(1)}, bf16[3,64,64]{2,1,0:T(8,128)(2,1)}, u32[]{:S(2)}) copy-start(bf16[3,64,64]{2,1,0:T(8,128)(2,1)} %get-tuple-element.342) | copy-start | bytes 73732 | tf_op jit(solution)/shard_map/while
  230.2 12.2 %collective-permute-start = (bf16[64,4096]{1,0:T(8,128)(2,1)S(1)}, bf16[64,4096]{1,0:T(8,128)(2,1)S(1)}, u32[]{:S(2)}, u32[]{:S(2)}) collective-permute-start(bf16[64,4096]{1,0:T(8,128)(2,1)S(1)} %fusion.101), channel_id=1, source_target_pairs={{2,0},{4,2},{6,4},{8,6},{10,8},{12,10},{14,12},{16,14},{18,16},{20... | collective-permute-start | bytes 1572872 | tf_op jit(solution)/shard_map/while/body/eval_jaxpr/ppermute | solution.py:16
  242.4 9.7 %copy-start = (bf16[64,4096]{1,0:T(8,128)(2,1)S(1)}, bf16[64,4096]{1,0:T(8,128)(2,1)}, u32[]{:S(2)}) copy-start(bf16[64,4096]{1,0:T(8,128)(2,1)} %get-tuple-element.343) | copy-start | bytes 1572868 | tf_op jit(solution)/shard_map/while
  242.4 9.7 %copy-start.1 = (bf16[3,64,64]{2,1,0:T(8,128)(2,1)S(1)}, bf16[3,64,64]{2,1,0:T(8,128)(2,1)}, u32[]{:S(2)}) copy-start(bf16[3,64,64]{2,1,0:T(8,128)(2,1)} %get-tuple-element.342) | copy-start | bytes 73732 | tf_op jit(solution)/shard_map/while
  252.4 11.6 %collective-permute-start = (bf16[64,4096]{1,0:T(8,128)(2,1)S(1)}, bf16[64,4096]{1,0:T(8,128)(2,1)S(1)}, u32[]{:S(2)}, u32[]{:S(2)}) collective-permute-start(bf16[64,4096]{1,0:T(8,128)(2,1)S(1)} %fusion.101), channel_id=1, source_target_pairs={{2,0},{4,2},{6,4},{8,6},{10,8},{12,10},{14,12},{16,14},{18,16},{20... | collective-permute-start | bytes 1572872 | tf_op jit(solution)/shard_map/while/body/eval_jaxpr/ppermute | solution.py:16
  264.0 11.5 %copy-start = (bf16[64,4096]{1,0:T(8,128)(2,1)S(1)}, bf16[64,4096]{1,0:T(8,128)(2,1)}, u32[]{:S(2)}) copy-start(bf16[64,4096]{1,0:T(8,128)(2,1)} %get-tuple-element.343) | copy-start | bytes 1572868 | tf_op jit(solution)/shard_map/while
  264.0 11.5 %copy-start.1 = (bf16[3,64,64]{2,1,0:T(8,128)(2,1)S(1)}, bf16[3,64,64]{2,1,0:T(8,128)(2,1)}, u32[]{:S(2)}) copy-start(bf16[3,64,64]{2,1,0:T(8,128)(2,1)} %get-tuple-element.342) | copy-start | bytes 73732 | tf_op jit(solution)/shard_map/while
  275.8 10.7 %collective-permute-start = (bf16[64,4096]{1,0:T(8,128)(2,1)S(1)}, bf16[64,4096]{1,0:T(8,128)(2,1)S(1)}, u32[]{:S(2)}, u32[]{:S(2)}) collective-permute-start(bf16[64,4096]{1,0:T(8,128)(2,1)S(1)} %fusion.101), channel_id=1, source_target_pairs={{2,0},{4,2},{6,4},{8,6},{10,8},{12,10},{14,12},{16,14},{18,16},{20... | collective-permute-start | bytes 1572872 | tf_op jit(solution)/shard_map/while/body/eval_jaxpr/ppermute | solution.py:16
  286.5 9.7 %copy-start = (bf16[64,4096]{1,0:T(8,128)(2,1)S(1)}, bf16[64,4096]{1,0:T(8,128)(2,1)}, u32[]{:S(2)}) copy-start(bf16[64,4096]{1,0:T(8,128)(2,1)} %get-tuple-element.343) | copy-start | bytes 1572868 | tf_op jit(solution)/shard_map/while
  286.5 9.7 %copy-start.1 = (bf16[3,64,64]{2,1,0:T(8,128)(2,1)S(1)}, bf16[3,64,64]{2,1,0:T(8,128)(2,1)}, u32[]{:S(2)}) copy-start(bf16[3,64,64]{2,1,0:T(8,128)(2,1)} %get-tuple-element.342) | copy-start | bytes 73732 | tf_op jit(solution)/shard_map/while
  296.5 10.8 %collective-permute-start = (bf16[64,4096]{1,0:T(8,128)(2,1)S(1)}, bf16[64,4096]{1,0:T(8,128)(2,1)S(1)}, u32[]{:S(2)}, u32[]{:S(2)}) collective-permute-start(bf16[64,4096]{1,0:T(8,128)(2,1)S(1)} %fusion.101), channel_id=1, source_target_pairs={{2,0},{4,2},{6,4},{8,6},{10,8},{12,10},{14,12},{16,14},{18,16},{20... | collective-permute-start | bytes 1572872 | tf_op jit(solution)/shard_map/while/body/eval_jaxpr/ppermute | solution.py:16
  307.3 11.5 %copy-start = (bf16[64,4096]{1,0:T(8,128)(2,1)S(1)}, bf16[64,4096]{1,0:T(8,128)(2,1)}, u32[]{:S(2)}) copy-start(bf16[64,4096]{1,0:T(8,128)(2,1)} %get-tuple-element.343) | copy-start | bytes 1572868 | tf_op jit(solution)/shard_map/while
  307.3 11.5 %copy-start.1 = (bf16[3,64,64]{2,1,0:T(8,128)(2,1)S(1)}, bf16[3,64,64]{2,1,0:T(8,128)(2,1)}, u32[]{:S(2)}) copy-start(bf16[3,64,64]{2,1,0:T(8,128)(2,1)} %get-tuple-element.342) | copy-start | bytes 73732 | tf_op jit(solution)/shard_map/while
  319.2 11.6 %collective-permute-start = (bf16[64,4096]{1,0:T(8,128)(2,1)S(1)}, bf16[64,4096]{1,0:T(8,128)(2,1)S(1)}, u32[]{:S(2)}, u32[]{:S(2)}) collective-permute-start(bf16[64,4096]{1,0:T(8,128)(2,1)S(1)} %fusion.101), channel_id=1, source_target_pairs={{2,0},{4,2},{6,4},{8,6},{10,8},{12,10},{14,12},{16,14},{18,16},{20... | collective-permute-start | bytes 1572872 | tf_op jit(solution)/shard_map/while/body/eval_jaxpr/ppermute | solution.py:16
  330.7 9.3 %copy-start = (bf16[64,4096]{1,0:T(8,128)(2,1)S(1)}, bf16[64,4096]{1,0:T(8,128)(2,1)}, u32[]{:S(2)}) copy-start(bf16[64,4096]{1,0:T(8,128)(2,1)} %get-tuple-element.343) | copy-start | bytes 1572868 | tf_op jit(solution)/shard_map/while
  330.7 9.3 %copy-start.1 = (bf16[3,64,64]{2,1,0:T(8,128)(2,1)S(1)}, bf16[3,64,64]{2,1,0:T(8,128)(2,1)}, u32[]{:S(2)}) copy-start(bf16[3,64,64]{2,1,0:T(8,128)(2,1)} %get-tuple-element.342) | copy-start | bytes 73732 | tf_op jit(solution)/shard_map/while
  340.3 13.2 %collective-permute-start = (bf16[64,4096]{1,0:T(8,128)(2,1)S(1)}, bf16[64,4096]{1,0:T(8,128)(2,1)S(1)}, u32[]{:S(2)}, u32[]{:S(2)}) collective-permute-start(bf16[64,4096]{1,0:T(8,128)(2,1)S(1)} %fusion.101), channel_id=1, source_target_pairs={{2,0},{4,2},{6,4},{8,6},{10,8},{12,10},{14,12},{16,14},{18,16},{20... | collective-permute-start | bytes 1572872 | tf_op jit(solution)/shard_map/while/body/eval_jaxpr/ppermute | solution.py:16
  353.5 10.2 %copy-start = (bf16[64,4096]{1,0:T(8,128)(2,1)S(1)}, bf16[64,4096]{1,0:T(8,128)(2,1)}, u32[]{:S(2)}) copy-start(bf16[64,4096]{1,0:T(8,128)(2,1)} %get-tuple-element.343) | copy-start | bytes 1572868 | tf_op jit(solution)/shard_map/while
  353.5 10.2 %copy-start.1 = (bf16[3,64,64]{2,1,0:T(8,128)(2,1)S(1)}, bf16[3,64,64]{2,1,0:T(8,128)(2,1)}, u32[]{:S(2)}) copy-start(bf16[3,64,64]{2,1,0:T(8,128)(2,1)} %get-tuple-element.342) | copy-start | bytes 73732 | tf_op jit(solution)/shard_map/while
  364.0 14.6 %collective-permute-start = (bf16[64,4096]{1,0:T(8,128)(2,1)S(1)}, bf16[64,4096]{1,0:T(8,128)(2,1)S(1)}, u32[]{:S(2)}, u32[]{:S(2)}) collective-permute-start(bf16[64,4096]{1,0:T(8,128)(2,1)S(1)} %fusion.101), channel_id=1, source_target_pairs={{2,0},{4,2},{6,4},{8,6},{10,8},{12,10},{14,12},{16,14},{18,16},{20... | collective-permute-start | bytes 1572872 | tf_op jit(solution)/shard_map/while/body/eval_jaxpr/ppermute | solution.py:16
  378.7 12.8 %copy-start = (bf16[64,4096]{1,0:T(8,128)(2,1)S(1)}, bf16[64,4096]{1,0:T(8,128)(2,1)}, u32[]{:S(2)}) copy-start(bf16[64,4096]{1,0:T(8,128)(2,1)} %get-tuple-element.343) | copy-start | bytes 1572868 | tf_op jit(solution)/shard_map/while
  378.7 12.8 %copy-start.1 = (bf16[3,64,64]{2,1,0:T(8,128)(2,1)S(1)}, bf16[3,64,64]{2,1,0:T(8,128)(2,1)}, u32[]{:S(2)}) copy-start(bf16[3,64,64]{2,1,0:T(8,128)(2,1)} %get-tuple-element.342) | copy-start | bytes 73732 | tf_op jit(solution)/shard_map/while
  391.8 15.0 %collective-permute-start = (bf16[64,4096]{1,0:T(8,128)(2,1)S(1)}, bf16[64,4096]{1,0:T(8,128)(2,1)S(1)}, u32[]{:S(2)}, u32[]{:S(2)}) collective-permute-start(bf16[64,4096]{1,0:T(8,128)(2,1)S(1)} %fusion.101), channel_id=1, source_target_pairs={{2,0},{4,2},{6,4},{8,6},{10,8},{12,10},{14,12},{16,14},{18,16},{20... | collective-permute-start | bytes 1572872 | tf_op jit(solution)/shard_map/while/body/eval_jaxpr/ppermute | solution.py:16
  406.8 10.2 %copy-start = (bf16[64,4096]{1,0:T(8,128)(2,1)S(1)}, bf16[64,4096]{1,0:T(8,128)(2,1)}, u32[]{:S(2)}) copy-start(bf16[64,4096]{1,0:T(8,128)(2,1)} %get-tuple-element.343) | copy-start | bytes 1572868 | tf_op jit(solution)/shard_map/while
  406.8 10.2 %copy-start.1 = (bf16[3,64,64]{2,1,0:T(8,128)(2,1)S(1)}, bf16[3,64,64]{2,1,0:T(8,128)(2,1)}, u32[]{:S(2)}) copy-start(bf16[3,64,64]{2,1,0:T(8,128)(2,1)} %get-tuple-element.342) | copy-start | bytes 73732 | tf_op jit(solution)/shard_map/while
  417.3 11.7 %collective-permute-start = (bf16[64,4096]{1,0:T(8,128)(2,1)S(1)}, bf16[64,4096]{1,0:T(8,128)(2,1)S(1)}, u32[]{:S(2)}, u32[]{:S(2)}) collective-permute-start(bf16[64,4096]{1,0:T(8,128)(2,1)S(1)} %fusion.101), channel_id=1, source_target_pairs={{2,0},{4,2},{6,4},{8,6},{10,8},{12,10},{14,12},{16,14},{18,16},{20... | collective-permute-start | bytes 1572872 | tf_op jit(solution)/shard_map/while/body/eval_jaxpr/ppermute | solution.py:16
  445.7 120.2 %copy-start.2 = (f32[1,1,64,256]{3,2,1,0:T(8,128)S(1)}, f32[1,1,64,256]{3,2,1,0:T(8,128)}, u32[]{:S(2)}) copy-start(f32[1,1,64,256]{3,2,1,0:T(8,128)} %param.15) | copy-start | bytes 196612
Sparse Core Ops, SparseCore 0:
  438.2 126.1 reduce-scatter.1
where the time goes:
time: 577 us; the launch traced here: 573 us
  waiting for transfers between devices  308 us (53%)
  blocking collectives  148 us (26%)
  matrix products  48.1 us (8%)
  other arithmetic  24.7 us (4%)
  starting transfers between devices  23.3 us (4%)
  between operations  14.8 us (3%)
    ppermute x18, waiting for transfers between devices, passed_along(): return lax.ppermute(block, axis, route)  191 us
    psum x18, blocking collectives, relay_tick(): hidden_grad = lax.psum(partial_hidden, 'tensor')  148 us
    reduce_scatter x1, waiting for transfers between devices, local(): lax.psum_scatter(coeffs, 'replica', scatter_dimension=2, tiled=True)  117 us
    dot_general x18, matrix products, relay_tick(): lax.dot_general(grad_out, w_down, (((1,), (1,)), ((), ())), preferred_ele...  23.9 us
    ppermute x18, starting transfers between devices, passed_along(): return lax.ppermute(block, axis, route)  23.3 us
    select_n x18, other arithmetic, relay_tick(): grad_out = jnp.where(position == section_count - 1, entering, incoming)  20.8 us
  transfers between devices with their start and end apart: 19, of which 19 were waited for; matrix products, arithmetic and copies ran while one was open for 3% of the time, Pallas kernels for 0%

commit v1 on v0

v1 whole, which is shorter than its diff:
```python
import math

import jax
import jax.numpy as jnp
from jax import lax
from jax.experimental import pallas as pl
from jax.experimental.pallas import tpu as pltpu
from jax.sharding import PartitionSpec as P

SPAN = 64
LOW = 8
momentum_decay = 0.9
outer_rate = 0.7

SECTIONS = 16
REPLICAS = 16
BAND = 64
COLS = 4096
ROWS = 192
CHUNK = 16
CHUNKS = ROWS // CHUNK
PIECES = 4
WIDTH = COLS // PIECES
MESH = pl.DeviceIdType.MESH
HIGH = lax.Precision.HIGHEST
BF = jnp.bfloat16
F32 = jnp.float32


def dot(a, b, precision=None):
    return jnp.dot(a, b, preferred_element_type=F32, precision=precision)


def dot_t(a, b, precision=None):
    return lax.dot_general(
        a, b, (((1,), (1,)), ((), ())), preferred_element_type=F32, precision=precision
    )


def basis(freqs, position):
    turns = (freqs * (2 * position + 1)) & (4 * SPAN - 1)
    weight = jnp.where(freqs == 0, math.sqrt(1.0 / SPAN), math.sqrt(2.0 / SPAN))
    return weight * jnp.cos(turns.astype(F32) * (math.pi / (2 * SPAN)))


def freqs_along(freq_ref, row, which):
    out = jnp.zeros_like(which)
    for k in range(LOW):
        out = jnp.where(which == k, freq_ref[row, k], out)
    return out


def kernel(
    freq_ref, flag_ref, cot_hbm, pre_ref, up_hbm, down_hbm, acc_hbm, outer_ref,
    res_ref, new_ref, step_ref,
    cot, wu, wd, acc, g, out, wd1, wd2, wu1, z, zsend, zbase, q, qsend, m1, m2, m1s, m2s, mcat,
    slope, hidden, coef, heard,
    load_sem, up1_s, up1_r, up2_s, up2_r, dn_s, dn_r, m1_s, m1_r, m2_s, m2_r, zb_s, zb_r,
    z_s, z_r, q_s, q_r, g_s, g_r, c_s, c_r,
):
    r = lax.axis_index("replica")
    s = lax.axis_index("section")
    t = lax.axis_index("tensor")
    other = 1 - t

    def sec(offset):
        return lax.rem(s + offset + SECTIONS, SECTIONS)

    def remote(src, dst, send, recv, section, tensor):
        return pltpu.make_async_remote_copy(
            src, dst, send, recv, device_id=(r, section, tensor), device_id_type=MESH
        )

    loads = [
        pltpu.make_async_copy(src, dst, load_sem.at[k])
        for k, (src, dst) in enumerate(
            ((down_hbm, wd), (cot_hbm, cot), (up_hbm, wu), (acc_hbm, acc))
        )
    ]
    for load in loads:
        load.start()

    barrier = pltpu.get_barrier_semaphore()
    for offset in (-2, -1, 1, 2):
        for tensor in range(2):
            pl.semaphore_signal(
                barrier, inc=1, device_id=(r, sec(offset), tensor), device_id_type=MESH
            )
    pl.semaphore_signal(barrier, inc=1, device_id=(r, s, other), device_id_type=MESH)
    for d in range(1, REPLICAS):
        pl.semaphore_signal(
            barrier, inc=1, device_id=(lax.rem(r + d, REPLICAS), s, t), device_id_type=MESH
        )
    pl.semaphore_wait(barrier, 9 + REPLICAS - 1)

    def cols(p):
        return pl.ds(p * WIDTH, WIDTH)

    up1 = [
        remote(down_hbm.at[:, cols(p)], wd1.at[:, cols(p)], up1_s.at[p], up1_r.at[p], sec(1), t)
        for p in range(PIECES)
    ]
    up2 = [
        remote(wd1.at[:, cols(p)], wd2.at[:, cols(p)], up2_s.at[p], up2_r.at[p], sec(1), t)
        for p in range(PIECES)
    ]
    dn = remote(up_hbm, wu1, dn_s, dn_r, sec(-1), t)
    for copy in up1:
        copy.start()
    dn.start()

    pre = pre_ref[...].astype(F32)
    sigma = jax.nn.sigmoid(pre)
    slope[...] = sigma * (1.0 + pre * (1.0 - sigma))
    hidden[...] = (pre * sigma).astype(BF)

    loads[0].wait()
    loads[1].wait()
    base_copy = remote(zbase, z.at[t], zb_s, zb_r, s, other)

    @pl.when(s >= SECTIONS - 3)
    def _():
        base = dot_t(cot[...], wd[...])
        zbase[...] = base
        base_copy.start()
        z[t] = base

    @pl.when(s == SECTIONS - 1)
    def _():
        g[...] = cot[...]
        q[...] = jnp.zeros_like(q)

    loads[2].wait()
    loads[3].wait()

    for p in range(PIECES):
        up1[p].wait_recv()
        up2[p].start()
    dn.wait_recv()
    m1s[...] = dot_t(wu[...], wd1[...])
    m2s[...] = dot_t(wu1[...], wd1[...])
    m1_copy = remote(m1s, m1.at[t], m1_s, m1_r, s, other)
    m2_copy = [remote(m2s, m2.at[t], m2_s.at[k], m2_r.at[t], sec(1), k) for k in range(2)]
    m2_from = [remote(m2s, m2.at[k], m2_s.at[k], m2_r.at[k], sec(1), k) for k in range(2)]
    m1_copy.start()
    for copy in m2_copy:
        copy.start()

    @pl.when(s >= SECTIONS - 3)
    def _():
        base_copy.wait()

    m1_copy.wait_recv()
    for copy in m2_from:
        copy.wait_recv()
    mcat[...] = jnp.concatenate([m1s[...] + m1[other], m2[0] + m2[1]], axis=1).astype(BF)

    def chunk_of(i):
        return pl.ds(pl.multiple_of(i * CHUNK, CHUNK), CHUNK)

    def q_copy(i):
        rows = chunk_of(i)
        return remote(qsend.at[rows], q.at[rows], q_s.at[i], q_r.at[i], sec(-1), t)

    def z_copy(i, k):
        rows = chunk_of(i)
        return remote(zsend.at[rows], z.at[t, rows], z_s.at[i, k], z_r.at[i, t], sec(-2), k)

    def z_from(i, k):
        rows = chunk_of(i)
        return remote(zsend.at[rows], z.at[k, rows], z_s.at[i, k], z_r.at[i, k], sec(-2), k)

    def g_copy(i, p):
        at = (chunk_of(i), cols(p))
        return remote(out.at[at], g.at[at], g_s.at[i, p], g_r.at[i, p], sec(-1), t)

    sends_q = s >= 2
    sends_z = jnp.logical_and(s >= 3, s <= SECTIONS - 2)

    def relay(i, _):
        rows = chunk_of(i)

        @pl.when(s >= 1)
        def _():
            @pl.when(s <= SECTIONS - 4)
            def _():
                z_from(i, 0).wait_recv()
                z_from(i, 1).wait_recv()

            @pl.when(s <= SECTIONS - 2)
            def _():
                q_copy(i).wait_recv()

            arrived = q[rows]
            total = z[0, rows] + z[1, rows] + arrived[:, :BAND]
            pre_grad = (total * slope[rows]).astype(BF)

            @pl.when(sends_q)
            def _():
                moved = jnp.concatenate(
                    [arrived[:, BAND:], jnp.zeros((CHUNK, BAND), F32)], axis=1
                )
                qsend[rows] = moved + dot(pre_grad, mcat[...])
                q_copy(i).start()

            for p in range(PIECES):
                @pl.when(s <= SECTIONS - 2)
                def _():
                    g_copy(i, p).wait_recv()

                passed = g[rows, cols(p)].astype(F32) + dot(pre_grad, wu[:, cols(p)])
                out[rows, cols(p)] = passed.astype(BF)
                g_copy(i, p).start()

        @pl.when(s == 0)
        def _():
            for p in range(PIECES):
                g_copy(i, p).wait_recv()

        @pl.when(sends_z)
        def _():
            @pl.when(i == 0)
            def _():
                for p in range(PIECES):
                    up2[p].wait_recv()

            zsend[rows] = dot_t(g[rows], wd2[...])
            for k in range(2):
                z_copy(i, k).start()

        return 0

    lax.fori_loop(0, CHUNKS, relay, 0)

    u_of = lax.broadcasted_iota(jnp.int32, (LOW, SPAN), 0)
    n_of = lax.broadcasted_iota(jnp.int32, (LOW, SPAN), 1)
    row_basis = basis(freqs_along(freq_ref, 0, u_of), n_of)
    u_t = lax.broadcasted_iota(jnp.int32, (SPAN, LOW), 1)
    n_t = lax.broadcasted_iota(jnp.int32, (SPAN, LOW), 0)
    row_basis_t = basis(freqs_along(freq_ref, 0, u_t), n_t)
    at_row = lax.broadcasted_iota(jnp.int32, (2 * SPAN, 2 * SPAN), 0)
    at_col = lax.broadcasted_iota(jnp.int32, (2 * SPAN, 2 * SPAN), 1)
    pair_basis = jnp.where(
        at_col // LOW == at_row // SPAN,
        basis(freqs_along(freq_ref, 1, lax.rem(at_col, LOW)), lax.rem(at_row, SPAN)),
        0.0,
    )

    grad = lax.dot_general(
        hidden[...], g[...], (((0,), (0,)), ((), ())), preferred_element_type=F32
    )
    moment = acc[...] + grad
    acc[...] = moment
    half = dot(row_basis, moment, HIGH)
    stacked = jnp.concatenate(
        [half[:, k * 2 * SPAN : (k + 1) * 2 * SPAN] for k in range(COLS // (2 * SPAN))], axis=0
    )
    coeffs = dot(stacked, pair_basis, HIGH)
    coef[...] = coeffs

    def share(k):
        return pl.ds(pl.multiple_of(k * 2 * LOW, 2 * LOW), 2 * LOW)

    def c_copy(d):
        to = lax.rem(r + d, REPLICAS)
        return pltpu.make_async_remote_copy(
            coef.at[share(to)], heard.at[d], c_s.at[d], c_r.at[d],
            device_id=(to, s, t), device_id_type=MESH,
        )

    for d in range(1, REPLICAS):
        c_copy(d).start()
    heard[0] = coef[share(r)]

    synced = flag_ref[0] == 1
    back = dot_t(coeffs, pair_basis, HIGH)
    wide = jnp.concatenate(
        [back[k * LOW : (k + 1) * LOW] for k in range(COLS // (2 * SPAN))], axis=1
    )
    decoded = dot(row_basis_t, wide, HIGH)
    moment = acc[...]
    res_ref[...] = jnp.where(synced, moment - decoded, moment)

    for p in range(PIECES):
        up1[p].wait_send()
        up2[p].wait_send()
    dn.wait_send()
    m1_copy.wait_send()
    for copy in m2_copy:
        copy.wait_send()

    @pl.when(jnp.logical_not(sends_z))
    def _():
        for p in range(PIECES):
            up2[p].wait_recv()

    def drain(i, _):
        @pl.when(sends_q)
        def _():
            q_copy(i).wait_send()

        @pl.when(sends_z)
        def _():
            for k in range(2):
                z_copy(i, k).wait_send()

        @pl.when(s >= 1)
        def _():
            for p in range(PIECES):
                g_copy(i, p).wait_send()

        return 0

    lax.fori_loop(0, CHUNKS, drain, 0)

    for d in range(1, REPLICAS):
        c_copy(d).wait_recv()
    summed = heard[0]
    for d in range(1, REPLICAS):
        summed = summed + heard[d]
    mean = summed * (1.0 / REPLICAS)
    back = dot_t(mean, pair_basis, HIGH)
    wide = jnp.concatenate([back[:LOW], back[LOW:]], axis=1)
    change = dot(row_basis_t, wide, HIGH)
    prior = outer_ref[...]
    moved = momentum_decay * prior + change
    stepped = -outer_rate * (change + momentum_decay * moved)
    new_ref[...] = jnp.where(synced, moved, prior)
    step_ref[...] = jnp.where(synced, stepped, jnp.zeros_like(stepped))
    for d in range(1, REPLICAS):
        c_copy(d).wait_send()


def local(
    cotangent, saved_pre, up_band, down_band, accumulated, outer_momentum, band_freqs, sync_flags
):
    vmem = pl.BlockSpec(memory_space=pltpu.VMEM)
    smem = pl.BlockSpec(memory_space=pltpu.SMEM)
    hbm = pl.BlockSpec(memory_space=pl.ANY)
    share = COLS // REPLICAS
    dma = pltpu.SemaphoreType.DMA
    residual, new_outer, outer_step = pl.pallas_call(
        kernel,
        out_shape=(
            jax.ShapeDtypeStruct((BAND, COLS), F32),
            jax.ShapeDtypeStruct((BAND, share), F32),
            jax.ShapeDtypeStruct((BAND, share), F32),
        ),
        in_specs=[smem, smem, hbm, vmem, hbm, hbm, hbm, vmem],
        out_specs=(vmem, vmem, vmem),
        scratch_shapes=[
            pltpu.VMEM((ROWS, COLS), BF),
            pltpu.VMEM((BAND, COLS), BF),
            pltpu.VMEM((BAND, COLS), BF),
            pltpu.VMEM((BAND, COLS), F32),
            pltpu.VMEM((ROWS, COLS), BF),
            pltpu.VMEM((ROWS, COLS), BF),
            pltpu.VMEM((BAND, COLS), BF),
            pltpu.VMEM((BAND, COLS), BF),
            pltpu.VMEM((BAND, COLS), BF),
            pltpu.VMEM((2, ROWS, BAND), F32),
            pltpu.VMEM((ROWS, BAND), F32),
            pltpu.VMEM((ROWS, BAND), F32),
            pltpu.VMEM((ROWS, 2 * BAND), F32),
            pltpu.VMEM((ROWS, 2 * BAND), F32),
            pltpu.VMEM((2, BAND, BAND), F32),
            pltpu.VMEM((2, BAND, BAND), F32),
            pltpu.VMEM((BAND, BAND), F32),
            pltpu.VMEM((BAND, BAND), F32),
            pltpu.VMEM((BAND, 2 * BAND), BF),
            pltpu.VMEM((ROWS, BAND), F32),
            pltpu.VMEM((ROWS, BAND), BF),
            pltpu.VMEM((REPLICAS * 2 * LOW, 2 * SPAN), F32),
            pltpu.VMEM((REPLICAS, 2 * LOW, 2 * SPAN), F32),
            dma((4,)),
            dma((PIECES,)), dma((PIECES,)), dma((PIECES,)), dma((PIECES,)),
            dma, dma, dma, dma,
            dma((2,)), dma((2,)),
            dma, dma,
            dma((CHUNKS, 2)), dma((CHUNKS, 2)),
            dma((CHUNKS,)), dma((CHUNKS,)),
            dma((CHUNKS, PIECES)), dma((CHUNKS, PIECES)),
            dma((REPLICAS,)), dma((REPLICAS,)),
        ],
        compiler_params=pltpu.CompilerParams(
            collective_id=0, has_side_effects=True, vmem_limit_bytes=48 << 20
        ),
        name="relay",
    )(
        band_freqs,
        sync_flags,
        cotangent.reshape(ROWS, COLS),
        saved_pre.reshape(ROWS, BAND),
        up_band[0],
        down_band[0],
        accumulated[0],
        outer_momentum[0, 0],
    )
    return (residual[None], new_outer[None, None], outer_step[None, None])


def solution(mesh):
    return jax.shard_map(
        local,
        mesh=mesh,
        in_specs=(
            P("replica", None, None, "tensor"),
            P("replica", "section", None, None, None),
            P("replica", "section", "tensor"),
            P("replica", "section", "tensor"),
            P("replica", "section", "tensor"),
            P("section", "tensor", None, "replica"),
            P(),
            P("section"),
        ),
        out_specs=(
            P("replica", "section", "tensor"),
            P("section", "tensor", None, "replica"),
            P("section", "tensor", None, "replica"),
        ),
        check_vma=False,
    )
```

time: 577 us -> 155 us (0.27)
  waiting for transfers between devices: 308 us -> 0 us
  blocking collectives: 148 us -> 0 us
  Pallas kernels: 0 us -> 144 us
  matrix products: 48.1 us -> 0 us
  other arithmetic: 24.7 us -> 0 us
  starting transfers between devices: 23.3 us -> 0 us
  between operations: 14.8 us -> 1.3 us
    ppermute x18 -> x0, waiting for transfers between devices: 191 us -> none  [passed_along(): return lax.ppermute(block, axis, route)]
    psum x18 -> x0, blocking collectives: 148 us -> none  [relay_tick(): hidden_grad = lax.psum(partial_hidden, 'tensor')]
    pallas_call x0 -> x1, Pallas kernels: none -> 144 us  [local(): pl.pallas_call(kernel, out_shape=(jax.ShapeDtypeStruct((BAND, COLS), F32)...]
    reduce_scatter x1 -> x0, waiting for transfers between devices: 117 us -> none  [local(): lax.psum_scatter(coeffs, 'replica', scatter_dimension=2, tiled=True)]
    dot_general x60 -> x0, matrix products: 48.1 us -> none  [the longest x18 23.9 us: relay_tick(): lax.dot_general(grad_out, w_down, (((1,), (1,)), ((), ())), preferred_ele...]
    ppermute x18 -> x0, starting transfers between devices: 23.3 us -> none  [passed_along(): return lax.ppermute(block, axis, route)]
    select_n x20 -> x0, other arithmetic: 22.2 us -> none  [the longest x18 20.8 us: relay_tick(): grad_out = jnp.where(position == section_count - 1, entering, incoming)]
    unnamed x2 -> x17, local copies, waits for them, and re-layouts: 0.01 us -> 9.25 us
  transfers between devices with their start and end apart: 19 -> 0, of which waited for: 19 -> 0; matrix products, arithmetic and copies ran while one was open for 3% -> 0% of each run, Pallas kernels for 0% -> 0%
where the time goes in v1:
time: 155 us
  Pallas kernels  144 us (93%)
  local copies, waits for them, and re-layouts  9.25 us (6%)
    pallas_call x1, Pallas kernels, local(): pl.pallas_call(kernel, out_shape=(jax.ShapeDtypeStruct((BAND, COLS), F32)...  144 us
    unnamed x17, local copies, waits for them, and re-layouts  9.25 us

profile of v1, /device:TPU:1, one launch (start us, length us, event | category | flops | bytes accessed | tf_op | source)
XLA Modules:
  0.0 154.8 jit_solution(1362833156694999147)
XLA Ops:
  1.3 0.0 copy-start
  1.3 1.4 copy-done
  2.7 0.0 copy-start.1
  2.7 1.2 copy-done.1
  3.9 0.0 copy-start.2
  3.9 1.0 copy-done.2
  5.0 0.0 copy-start.3
  5.0 1.0 copy-done.3
  6.0 0.0 copy-start.4
  6.0 0.8 copy-done.4
  6.8 0.0 copy-start.5
  6.8 0.8 copy-done.5
  7.6 0.0 copy-start.6
  7.6 0.7 copy-done.6
  8.3 144.2 %relay.1 = (f32[64,4096]{1,0:T(8,128)S(1)}, f32[64,256]{1,0:T(8,128)S(1)}, f32[64,256]{1,0:T(8,128)S(1)}) custom-call(s32[2,8]{1,0:T(2,128)S(1)} %copy-done.6, s32[1]{0:T(128)S(6)} %copy.14.flag_ref, bf16[192,4096]{1,0:T(8,128)(2,1)S(1)} %bitcast.9, bf16[192,64]{1,0:T(8,128)(2,1)S(1)} %bitcast.17, bf16[64,4096]{1,0:T(8,128)(2,1)S(1)} %bitcast.12, ...), custom_call_target="tpu_custom_call" | custom-call | tf_op jit(solution)/shard_map/relay/pallas_call | solution.py:342
  152.5 1.0 copy.15
  153.5 0.6 copy.16
  154.1 0.6 copy.17
Async XLA Ops:
  1.3 1.4 copy-start
  2.7 1.2 copy-start.1
  3.9 1.0 copy-start.2
  5.0 1.0 copy-start.3
  6.0 0.8 copy-start.4
  6.8 0.8 copy-start.5
  7.6 0.7 copy-start.6

commit v2 on v1

v2 whole, which is shorter than its diff:
```python
import math

import jax
import jax.numpy as jnp
from jax import lax
from jax.experimental import pallas as pl
from jax.experimental.pallas import tpu as pltpu
from jax.sharding import PartitionSpec as P

SPAN = 64
LOW = 8
momentum_decay = 0.9
outer_rate = 0.7

SECTIONS = 16
REPLICAS = 16
BAND = 64
COLS = 4096
ROWS = 192
CHUNK = 16
CHUNKS = ROWS // CHUNK
SHARE = COLS // (2 * SPAN) * LOW // REPLICAS
PIECES = 4
WIDTH = COLS // PIECES
PARTS = 4
PART = COLS // PARTS
HALF = CHUNK // 2
MESH = pl.DeviceIdType.MESH
HIGH = lax.Precision.HIGHEST
BF = jnp.bfloat16
F32 = jnp.float32


def dot(a, b, precision=None):
    return jnp.dot(a, b, preferred_element_type=F32, precision=precision)


def dot_t(a, b, precision=None):
    return lax.dot_general(
        a, b, (((1,), (1,)), ((), ())), preferred_element_type=F32, precision=precision
    )


def basis(freqs, position):
    turns = (freqs * (2 * position + 1)) & (4 * SPAN - 1)
    weight = jnp.where(freqs == 0, math.sqrt(1.0 / SPAN), math.sqrt(2.0 / SPAN))
    return weight * jnp.cos(turns.astype(F32) * (math.pi / (2 * SPAN)))


def freqs_along(freq_ref, row, which):
    out = jnp.zeros_like(which)
    for k in range(LOW):
        out = jnp.where(which == k, freq_ref[row, k], out)
    return out


def packed(block):
    return jnp.concatenate([block[:HALF], block[HALF:]], axis=1)


def unpacked(block):
    return jnp.concatenate([block[:, :BAND], block[:, BAND:]], axis=0)


def kernel(
    freq_ref, flag_ref, cot_hbm, pre_hbm, up_hbm, down_hbm, acc_hbm,
    delta_hbm, change_ref,
    cot, pre_ref, wu, wd, acc, g, out, wd1, wd2, wu1, z, za, zn, zf, q, qsend, m1, m2, m1s, m2s, near, far,
    slope, hidden, own, coef, heard,
    load_sem, up1_s, up1_r, up2_s, up2_r, dn_s, dn_r, m1_s, m1_r, m2_s, m2_r, zb_s, zb_r,
    za_s, zn_s, zf_s, z_r, q_s, q_r, g_s, g_r, c_s, c_r,
):
    r = lax.axis_index("replica")
    s = lax.axis_index("section")
    t = lax.axis_index("tensor")
    other = 1 - t
    top = SECTIONS - 1

    def sec(offset):
        return lax.rem(s + offset + SECTIONS, SECTIONS)

    def remote(src, dst, send, recv, section, tensor):
        return pltpu.make_async_remote_copy(
            src, dst, send, recv, device_id=(r, section, tensor), device_id_type=MESH
        )

    loads = [
        pltpu.make_async_copy(src, dst, load_sem.at[k])
        for k, (src, dst) in enumerate(
            (
                (pre_hbm, pre_ref),
                (down_hbm, wd),
                (cot_hbm, cot),
                (up_hbm, wu),
                (acc_hbm, acc),
            )
        )
    ]
    for load in loads:
        load.start()

    barrier = pltpu.get_barrier_semaphore()
    for offset in (-2, -1, 1, 2):
        for tensor in range(2):
            pl.semaphore_signal(
                barrier, inc=1, device_id=(r, sec(offset), tensor), device_id_type=MESH
            )
    pl.semaphore_signal(barrier, inc=1, device_id=(r, s, other), device_id_type=MESH)
    for d in range(1, REPLICAS):
        pl.semaphore_signal(
            barrier, inc=1, device_id=(lax.rem(r + d, REPLICAS), s, t), device_id_type=MESH
        )
    pl.semaphore_wait(barrier, 9 + REPLICAS - 1)

    def part(p):
        return pl.ds(p * PART, PART)

    up1 = [
        remote(down_hbm.at[:, part(p)], wd1.at[:, part(p)], up1_s.at[p], up1_r.at[p], sec(1), t)
        for p in range(PARTS)
    ]
    up2 = [
        remote(wd1.at[:, part(p)], wd2.at[:, part(p)], up2_s.at[p], up2_r.at[p], sec(1), t)
        for p in range(PARTS)
    ]
    dn = remote(up_hbm, wu1, dn_s, dn_r, sec(-1), t)
    for copy in up1:
        copy.start()
    dn.start()

    for load in loads[:4]:
        load.wait()
    base_copy = remote(za, z.at[t], zb_s, zb_r, s, other)

    @pl.when(s == top)
    def _():
        base = dot_t(cot[...], wd[...])
        for i in range(CHUNKS):
            za[pl.ds(i * HALF, HALF)] = packed(base[i * CHUNK : (i + 1) * CHUNK])
        base_copy.start()
        z[t] = za[...]

    pre = pre_ref[...].astype(F32)
    sigma = jax.nn.sigmoid(pre)
    slope[...] = sigma * (1.0 + pre * (1.0 - sigma))
    hidden[...] = (pre * sigma).astype(BF)

    def cols(p):
        return pl.ds(p * WIDTH, WIDTH)

    def chunk_of(i):
        return pl.ds(pl.multiple_of(i * CHUNK, CHUNK), CHUNK)

    def half_of(i):
        return pl.ds(pl.multiple_of(i * HALF, HALF), HALF)

    def q_copy(i):
        rows = half_of(i)
        return remote(qsend.at[rows], q.at[rows], q_s.at[i], q_r.at[i], sec(-1), t)

    def za_copy(i):
        rows = half_of(i)
        return remote(za.at[rows], z.at[t, rows], za_s.at[i], z_r.at[i, t], s, other)

    def zn_copy(i, k):
        rows = half_of(i)
        return remote(zn.at[rows], z.at[t, rows], zn_s.at[i, k], z_r.at[i, t], sec(-1), k)

    def zf_copy(i, k):
        rows = half_of(i)
        return remote(zf.at[rows], z.at[t, rows], zf_s.at[i, k], z_r.at[i, t], sec(-2), k)

    def z_from(i, k):
        rows = half_of(i)
        return remote(zf.at[rows], z.at[k, rows], zf_s.at[i, k], z_r.at[i, k], sec(-2), k)

    def g_copy(i, p):
        at = (chunk_of(i), cols(p))
        return remote(out.at[at], g.at[at], g_s.at[i, p], g_r.at[i, p], sec(-1), t)

    def add_own(i, p, entering, pre_grad):
        passed = entering.astype(F32) + own[:, cols(p)]
        out[chunk_of(i), cols(p)] = passed.astype(BF)
        g_copy(i, p).start()

    def pre_grad_of(i, from_above):
        total = z[0, half_of(i)] + z[1, half_of(i)]
        if from_above:
            total = total + q[half_of(i)]
        pre_grad = (unpacked(total) * slope[chunk_of(i)]).astype(BF)
        own[...] = dot(pre_grad, wu[...])
        return pre_grad

    def send_q(i, pre_grad):
        qsend[half_of(i)] = packed(dot(pre_grad, near[...]))
        q_copy(i).start()

    def send_near(i):
        zn[half_of(i)] = packed(dot_t(g[chunk_of(i)], wd1[...]))
        for k in range(2):
            zn_copy(i, k).start()

    @pl.when(s == top)
    def _():
        base_copy.wait()

        def first(i, _):
            pre_grad = pre_grad_of(i, False)
            for p in range(PIECES):
                add_own(i, p, cot[chunk_of(i), cols(p)], pre_grad)
            return 0

        lax.fori_loop(0, CHUNKS, first, 0)
        g[...] = cot[...]

    def own_base(i):
        for p in range(PIECES):
            g_copy(i, p).wait_recv()
        part_sum = packed(dot_t(g[chunk_of(i)], wd[...]))
        za[half_of(i)] = part_sum
        za_copy(i).start()
        z[t, half_of(i)] = part_sum

    def second(i):
        remote(za.at[half_of(i)], z.at[other, half_of(i)], za_s.at[i], z_r.at[i, other], s, other).wait_recv()
        pre_grad = pre_grad_of(i, False)
        for p in range(PIECES):
            add_own(i, p, g[chunk_of(i), cols(p)], pre_grad)
        return pre_grad

    @pl.when(s == top - 1)
    def _():
        own_base(0)
        own_base(1)

    for p in range(PARTS):
        up1[p].wait_recv()
        up2[p].start()
    m1s[...] = dot_t(wu[...], wd1[...])
    m1_copy = remote(m1s, m1.at[t], m1_s, m1_r, s, other)
    m1_copy.start()

    @pl.when(s == top - 1)
    def _():
        send_near(0)
        send_near(1)

    dn.wait_recv()
    m2s[...] = dot_t(wu1[...], wd1[...])
    m2_copy = [remote(m2s, m2.at[t], m2_s.at[k], m2_r.at[t], sec(1), k) for k in range(2)]
    m2_from = [remote(m2s, m2.at[k], m2_s.at[k], m2_r.at[k], sec(1), k) for k in range(2)]
    for copy in m2_copy:
        copy.start()

    @pl.when(s == top - 1)
    def _():
        qsend[half_of(0)] = packed(second(0).astype(F32))
        own_base(2)
        send_near(2)

    m1_copy.wait_recv()
    near[...] = (m1s[...] + m1[other]).astype(BF)

    @pl.when(s == top - 1)
    def _():
        send_q(0, unpacked(qsend[half_of(0)]).astype(BF))

        def rest(i, _):
            send_q(i, second(i))

            @pl.when(i < CHUNKS - 2)
            def _():
                own_base(i + 2)
                send_near(i + 2)

            return 0

        lax.fori_loop(1, CHUNKS, rest, 0)

    for copy in m2_from:
        copy.wait_recv()
    far[...] = (0.5 * (m2[0] + m2[1])).astype(BF)

    sends_q = jnp.logical_and(s >= 2, s <= top - 1)
    sends_near = jnp.logical_or(s == top - 1, s == top - 2)
    sends_far = jnp.logical_and(s >= 3, s <= top - 2)

    def relay(i, _):
        z_from(i, 0).wait_recv()
        z_from(i, 1).wait_recv()
        q_copy(i).wait_recv()
        pre_grad = pre_grad_of(i, True)

        @pl.when(s >= 2)
        def _():
            send_q(i, pre_grad)

        @pl.when(jnp.logical_and(s != top - 2, i == 0))
        def _():
            for p in range(PARTS):
                up2[p].wait_recv()

        for p in range(PIECES):
            g_copy(i, p).wait_recv()
            add_own(i, p, g[chunk_of(i), cols(p)], pre_grad)

        @pl.when(s == top - 2)
        def _():
            send_near(i)

            @pl.when(i == 0)
            def _():
                for p in range(PARTS):
                    up2[p].wait_recv()

        @pl.when(s >= 3)
        def _():
            ahead = dot(pre_grad, far[...]) + dot_t(g[chunk_of(i)], wd2[...])
            zf[half_of(i)] = packed(ahead)
            for k in range(2):
                zf_copy(i, k).start()

        return 0

    @pl.when(jnp.logical_and(s >= 1, s <= top - 2))
    def _():
        lax.fori_loop(0, CHUNKS, relay, 0)

    @pl.when(s == 0)
    def _():
        def last(i, _):
            for p in range(PIECES):
                g_copy(i, p).wait_recv()
            return 0

        lax.fori_loop(0, CHUNKS, last, 0)

    u_of = lax.broadcasted_iota(jnp.int32, (LOW, SPAN), 0)
    n_of = lax.broadcasted_iota(jnp.int32, (LOW, SPAN), 1)
    row_basis = basis(freqs_along(freq_ref, 0, u_of), n_of)
    u_t = lax.broadcasted_iota(jnp.int32, (SPAN, LOW), 1)
    n_t = lax.broadcasted_iota(jnp.int32, (SPAN, LOW), 0)
    row_basis_t = basis(freqs_along(freq_ref, 0, u_t), n_t)
    at_row = lax.broadcasted_iota(jnp.int32, (2 * SPAN, 2 * SPAN), 0)
    at_col = lax.broadcasted_iota(jnp.int32, (2 * SPAN, 2 * SPAN), 1)
    pair_basis = jnp.where(
        at_col // LOW == at_row // SPAN,
        basis(freqs_along(freq_ref, 1, lax.rem(at_col, LOW)), lax.rem(at_row, SPAN)),
        0.0,
    )

    loads[4].wait()
    grad = lax.dot_general(
        hidden[...], g[...], (((0,), (0,)), ((), ())), preferred_element_type=F32
    )
    moment = acc[...] + grad
    half = dot(row_basis, moment, HIGH)
    acc[...] = grad
    stacked = jnp.concatenate(
        [half[:, k * 2 * SPAN : (k + 1) * 2 * SPAN] for k in range(COLS // (2 * SPAN))], axis=0
    )
    coeffs = dot(stacked, pair_basis, HIGH)
    coef[...] = coeffs

    def share(k):
        return pl.ds(pl.multiple_of(k * SHARE, SHARE), SHARE)

    def c_copy(d):
        to = lax.rem(r + d, REPLICAS)
        return pltpu.make_async_remote_copy(
            coef.at[share(to)], heard.at[d], c_s.at[d], c_r.at[d],
            device_id=(to, s, t), device_id_type=MESH,
        )

    for d in range(1, REPLICAS):
        c_copy(d).start()
    heard[0] = coef[share(r)]

    synced = flag_ref[0] == 1
    back = dot_t(coeffs, pair_basis, HIGH)
    wide = jnp.concatenate(
        [back[k * LOW : (k + 1) * LOW] for k in range(COLS // (2 * SPAN))], axis=1
    )
    decoded = dot(row_basis_t, wide, HIGH)
    acc[...] = jnp.where(synced, acc[...] - decoded, acc[...])
    store = pltpu.make_async_copy(acc, delta_hbm, load_sem.at[5])
    store.start()

    for p in range(PARTS):
        up1[p].wait_send()
        up2[p].wait_send()
    dn.wait_send()
    m1_copy.wait_send()
    for copy in m2_copy:
        copy.wait_send()

    @pl.when(jnp.logical_not(sends_far))
    def _():
        @pl.when(jnp.logical_not(jnp.logical_and(s >= 1, s <= top - 2)))
        def _():
            for p in range(PARTS):
                up2[p].wait_recv()

    def drain(i, _):
        @pl.when(s == top - 1)
        def _():
            za_copy(i).wait_send()

        @pl.when(sends_near)
        def _():
            for k in range(2):
                zn_copy(i, k).wait_send()

        @pl.when(sends_far)
        def _():
            for k in range(2):
                zf_copy(i, k).wait_send()

        @pl.when(sends_q)
        def _():
            q_copy(i).wait_send()

        @pl.when(s >= 1)
        def _():
            for p in range(PIECES):
                g_copy(i, p).wait_send()

        return 0

    lax.fori_loop(0, CHUNKS, drain, 0)

    for d in range(1, REPLICAS):
        c_copy(d).wait_recv()
    summed = heard[0]
    for d in range(1, REPLICAS):
        summed = summed + heard[d]
    mean = summed * (1.0 / REPLICAS)
    back = dot_t(mean, pair_basis, HIGH)
    wide = jnp.concatenate([back[k * LOW : (k + 1) * LOW] for k in range(SHARE // LOW)], axis=1)
    change_ref[...] = dot(row_basis_t, wide, HIGH)
    store.wait()
    for d in range(1, REPLICAS):
        c_copy(d).wait_send()


def local(
    cotangent, saved_pre, up_band, down_band, accumulated, outer_momentum, band_freqs, sync_flags
):
    vmem = pl.BlockSpec(memory_space=pltpu.VMEM)
    smem = pl.BlockSpec(memory_space=pltpu.SMEM)
    hbm = pl.BlockSpec(memory_space=pl.ANY)
    share = COLS // REPLICAS
    dma = pltpu.SemaphoreType.DMA
    half_rows = ROWS // 2
    delta, change = pl.pallas_call(
        kernel,
        out_shape=(
            jax.ShapeDtypeStruct((BAND, COLS), F32),
            jax.ShapeDtypeStruct((BAND, share), F32),
        ),
        in_specs=[smem, smem, hbm, hbm, hbm, hbm, hbm],
        out_specs=(hbm, vmem),
        scratch_shapes=[
            pltpu.VMEM((ROWS, COLS), BF),
            pltpu.VMEM((ROWS, BAND), BF),
            pltpu.VMEM((BAND, COLS), BF),
            pltpu.VMEM((BAND, COLS), BF),
            pltpu.VMEM((BAND, COLS), F32),
            pltpu.VMEM((ROWS, COLS), BF),
            pltpu.VMEM((ROWS, COLS), BF),
            pltpu.VMEM((BAND, COLS), BF),
            pltpu.VMEM((BAND, COLS), BF),
            pltpu.VMEM((BAND, COLS), BF),
            pltpu.VMEM((2, half_rows, 2 * BAND), F32),
            pltpu.VMEM((half_rows, 2 * BAND), F32),
            pltpu.VMEM((half_rows, 2 * BAND), F32),
            pltpu.VMEM((half_rows, 2 * BAND), F32),
            pltpu.VMEM((half_rows, 2 * BAND), F32),
            pltpu.VMEM((half_rows, 2 * BAND), F32),
            pltpu.VMEM((2, BAND, BAND), F32),
            pltpu.VMEM((2, BAND, BAND), F32),
            pltpu.VMEM((BAND, BAND), F32),
            pltpu.VMEM((BAND, BAND), F32),
            pltpu.VMEM((BAND, BAND), BF),
            pltpu.VMEM((BAND, BAND), BF),
            pltpu.VMEM((ROWS, BAND), F32),
            pltpu.VMEM((ROWS, BAND), BF),
            pltpu.VMEM((CHUNK, COLS), F32),
            pltpu.VMEM((REPLICAS * SHARE, 2 * SPAN), F32),
            pltpu.VMEM((REPLICAS, SHARE, 2 * SPAN), F32),
            dma((6,)),
            dma((PARTS,)), dma((PARTS,)), dma((PARTS,)), dma((PARTS,)),
            dma, dma, dma, dma,
            dma((2,)), dma((2,)),
            dma, dma,
            dma((CHUNKS,)), dma((CHUNKS, 2)), dma((CHUNKS, 2)), dma((CHUNKS, 2)),
            dma((CHUNKS,)), dma((CHUNKS,)),
            dma((CHUNKS, PIECES)), dma((CHUNKS, PIECES)),
            dma((REPLICAS,)), dma((REPLICAS,)),
        ],
        compiler_params=pltpu.CompilerParams(
            collective_id=0, has_side_effects=True, vmem_limit_bytes=60 << 20
        ),
        name="relay",
    )(
        band_freqs,
        sync_flags,
        cotangent.reshape(ROWS, COLS),
        saved_pre.reshape(ROWS, BAND),
        up_band[0],
        down_band[0],
        accumulated[0],
    )
    residual = accumulated + delta[None]
    synced = sync_flags[0] == 1
    prior = outer_momentum[0, 0]
    moved = momentum_decay * prior + change
    stepped = -outer_rate * (change + momentum_decay * moved)
    new_outer = jnp.where(synced, moved, prior)
    outer_step = jnp.where(synced, stepped, jnp.zeros_like(stepped))
    return (residual, new_outer[None, None], outer_step[None, None])


def solution(mesh):
    return jax.shard_map(
        local,
        mesh=mesh,
        in_specs=(
            P("replica", None, None, "tensor"),
            P("replica", "section", None, None, None),
            P("replica", "section", "tensor"),
            P("replica", "section", "tensor"),
            P("replica", "section", "tensor"),
            P("section", "tensor", None, "replica"),
            P(),
            P("section"),
        ),
        out_specs=(
            P("replica", "section", "tensor"),
            P("section", "tensor", None, "replica"),
            P("section", "tensor", None, "replica"),
        ),
        check_vma=False,
    )
```

time: 155 us -> 141 us (0.910)
  local copies, waits for them, and re-layouts: 9.25 us -> 0.01 us
  Pallas kernels: 144 us -> 137 us
  other arithmetic: 0 us -> 3.01 us
    unnamed x17 -> x6, local copies, waits for them, and re-layouts: 9.25 us -> 0.01 us
    pallas_call x1, Pallas kernels: 144 us -> 137 us  [local(): pl.pallas_call(kernel, out_shape=(jax.ShapeDtypeStruct((BAND, COLS), F32)...]
    add x0 -> x1, other arithmetic: none -> 2.34 us  [local(): residual = accumulated + delta[None]]
where the time goes in v2:
time: 141 us
  Pallas kernels  137 us (97%)
  other arithmetic  3.01 us (2%)
    pallas_call x1, Pallas kernels, local(): pl.pallas_call(kernel, out_shape=(jax.ShapeDtypeStruct((BAND, COLS), F32)...  137 us

profile of v2, /device:TPU:1, one launch (start us, length us, event | category | flops | bytes accessed | tf_op | source)
XLA Modules:
  0.0 141.3 jit_solution(13716149319162846419)
XLA Ops:
  1.3 0.0 copy-start
  1.3 137.0 %relay.1 = (f32[64,4096]{1,0:T(8,128)}, f32[64,256]{1,0:T(8,128)}) custom-call(s32[2,8]{1,0:T(2,128)} %freq_ref.1, s32[1]{0:T(128)S(6)} %copy.11.flag_ref, bf16[192,4096]{1,0:T(8,128)(2,1)} %bitcast.24, bf16[192,64]{1,0:T(8,128)(2,1)} %bitcast.27, bf16[64,4096]{1,0:T(8,128)(2,1)} %bitcast.25, bf16[64,4096]{1,0:T(8,128)(2,1)} %bitcast.26, f32[64,4096]{1,0:T(8,128)} %bitcast.23), custom_call_target="tpu_custom_call" | custom-call | tf_op jit(solution)/shard_map/relay/pallas_call | solution.py:455
  138.3 0.0 copy-done
  138.3 0.0 copy-start.1
  138.3 0.0 copy-start.2
  138.3 2.3 %bitcast_add_fusion = f32[1,64,4096]{2,1,0:T(8,128)} fusion(f32[1,64,4096]{2,1,0:T(8,128)S(1)} %copy-done, f32[64,4096]{1,0:T(8,128)} %get-tuple-element.5), kind=kLoop, calls=%fused_computation | loop fusion | flops 262144 | bytes 3145728 | tf_op jit(solution)/shard_map/add | solution.py:514
  140.7 0.0 copy-done.1
  140.7 0.0 copy-done.2
  140.7 0.7 select_bitcast_fusion
Async XLA Ops:
  1.3 137.0 %copy-start = (f32[1,64,4096]{2,1,0:T(8,128)S(1)}, f32[1,64,4096]{2,1,0:T(8,128)}, u32[]{:S(2)}) copy-start(f32[1,64,4096]{2,1,0:T(8,128)} %param.12) | copy-start | bytes 3145732
  138.3 2.4 %copy-start.1 = (f32[1,1,64,256]{3,2,1,0:T(8,128)S(1)}, f32[1,1,64,256]{3,2,1,0:T(8,128)}, u32[]{:S(2)}) copy-start(f32[1,1,64,256]{3,2,1,0:T(8,128)} %param.13) | copy-start | bytes 196612
  138.3 2.4 %copy-start.2 = (f32[64,256]{1,0:T(8,128)S(1)}, f32[64,256]{1,0:T(8,128)}, u32[]{:S(2)}) copy-start(f32[64,256]{1,0:T(8,128)} %get-tuple-element.6) | copy-start | bytes 196612

commit v3 on v2

--- a/solution.py
+++ b/solution.py
@@ -21,6 +21,9 @@
 CHUNKS = ROWS // CHUNK
 SHARE = COLS // (2 * SPAN) * LOW // REPLICAS
 PIECES = 4
+LIMIT = 60
+GROUPS = 3
+GROUP = ROWS // GROUPS
 WIDTH = COLS // PIECES
 PARTS = 4
 PART = COLS // PARTS
@@ -55,7 +58,7 @@
 
 
 def packed(block):
-    return jnp.concatenate([block[:HALF], block[HALF:]], axis=1)
+    return jnp.concatenate([block[:HALF], block[HALF:]], axis=1).astype(BF)
 
 
 def unpacked(block):
@@ -63,10 +66,11 @@
 
 
 def kernel(
-    freq_ref, flag_ref, cot_hbm, pre_hbm, up_hbm, down_hbm, acc_hbm,
-    delta_hbm, change_ref,
+    freq_hbm, flag_hbm, cot_hbm, pre_hbm, up_hbm, down_hbm, acc_hbm,
+    delta_ref, change_ref,
+    freq_ref, flag_ref, row_ref, row_t_ref, pair_ref,
     cot, pre_ref, wu, wd, acc, g, out, wd1, wd2, wu1, z, za, zn, zf, q, qsend, m1, m2, m1s, m2s, near, far,
-    slope, hidden, own, coef, heard,
+    slope, hidden, own, kept, coef, heard,
     load_sem, up1_s, up1_r, up2_s, up2_r, dn_s, dn_r, m1_s, m1_r, m2_s, m2_r, zb_s, zb_r,
     za_s, zn_s, zf_s, z_r, q_s, q_r, g_s, g_r, c_s, c_r,
 ):
@@ -93,6 +97,8 @@
                 (cot_hbm, cot),
                 (up_hbm, wu),
                 (acc_hbm, acc),
+                (freq_hbm, freq_ref),
+                (flag_hbm, flag_ref),
             )
         )
     ]
@@ -126,106 +132,136 @@
     dn = remote(up_hbm, wu1, dn_s, dn_r, sec(-1), t)
     for copy in up1:
         copy.start()
-    dn.start()
+
+    sends_dn = s <= top - 2
+    takes_dn = jnp.logical_or(s <= top - 3, s == top)
+
+    @pl.when(sends_dn)
+    def _():
+        dn.start()
 
     for load in loads[:4]:
         load.wait()
-    base_copy = remote(za, z.at[t], zb_s, zb_r, s, other)
+
+    def base_rows(k):
+        return pl.ds(k * (GROUP // CHUNK), GROUP // CHUNK)
+
+    base_copy = [
+        remote(za.at[base_rows(k)], z.at[t, base_rows(k)], zb_s.at[k], zb_r.at[k], s, other)
+        for k in range(GROUPS)
+    ]
+    base_from = [
+        remote(za.at[base_rows(k)], z.at[other, base_rows(k)], zb_s.at[k], zb_r.at[k], s, other)
+        for k in range(GROUPS)
+    ]
 
     @pl.when(s == top)
     def _():
-        base = dot_t(cot[...], wd[...])
-        for i in range(CHUNKS):
-            za[pl.ds(i * HALF, HALF)] = packed(base[i * CHUNK : (i + 1) * CHUNK])
-        base_copy.start()
-        z[t] = za[...]
+        for k in range(GROUPS):
+            base = dot_t(cot[pl.ds(k * GROUP, GROUP)], wd[...])
+            for i in range(GROUP // CHUNK):
+                za[k * (GROUP // CHUNK) + i] = packed(base[i * CHUNK : (i + 1) * CHUNK])
+            base_copy[k].start()
+            z[t, base_rows(k)] = za[base_rows(k)]
 
     pre = pre_ref[...].astype(F32)
     sigma = jax.nn.sigmoid(pre)
     slope[...] = sigma * (1.0 + pre * (1.0 - sigma))
     hidden[...] = (pre * sigma).astype(BF)
 
+    for load in loads[5:]:
+        load.wait()
+    u_of = lax.broadcasted_iota(jnp.int32, (LOW, SPAN), 0)
+    n_of = lax.broadcasted_iota(jnp.int32, (LOW, SPAN), 1)
+    row_ref[...] = basis(freqs_along(freq_ref, 0, u_of), n_of)
+    u_t = lax.broadcasted_iota(jnp.int32, (SPAN, LOW), 1)
+    n_t = lax.broadcasted_iota(jnp.int32, (SPAN, LOW), 0)
+    row_t_ref[...] = basis(freqs_along(freq_ref, 0, u_t), n_t)
+    at_row = lax.broadcasted_iota(jnp.int32, (2 * SPAN, 2 * SPAN), 0)
+    at_col = lax.broadcasted_iota(jnp.int32, (2 * SPAN, 2 * SPAN), 1)
+    pair_ref[...] = jnp.where(
+        at_col // LOW == at_row // SPAN,
+        basis(freqs_along(freq_ref, 1, lax.rem(at_col, LOW)), lax.rem(at_row, SPAN)),
+        0.0,
+    )
+
     def cols(p):
         return pl.ds(p * WIDTH, WIDTH)
 
     def chunk_of(i):
         return pl.ds(pl.multiple_of(i * CHUNK, CHUNK), CHUNK)
 
-    def half_of(i):
-        return pl.ds(pl.multiple_of(i * HALF, HALF), HALF)
-
     def q_copy(i):
-        rows = half_of(i)
-        return remote(qsend.at[rows], q.at[rows], q_s.at[i], q_r.at[i], sec(-1), t)
+        return remote(qsend.at[i], q.at[i], q_s.at[i], q_r.at[i], sec(-1), t)
 
     def za_copy(i):
-        rows = half_of(i)
-        return remote(za.at[rows], z.at[t, rows], za_s.at[i], z_r.at[i, t], s, other)
+        return remote(za.at[i], z.at[t, i], za_s.at[i], z_r.at[i, t], s, other)
 
     def zn_copy(i, k):
-        rows = half_of(i)
-        return remote(zn.at[rows], z.at[t, rows], zn_s.at[i, k], z_r.at[i, t], sec(-1), k)
+        return remote(zn.at[i], z.at[t, i], zn_s.at[i, k], z_r.at[i, t], sec(-1), k)
 
     def zf_copy(i, k):
-        rows = half_of(i)
-        return remote(zf.at[rows], z.at[t, rows], zf_s.at[i, k], z_r.at[i, t], sec(-2), k)
+        return remote(zf.at[i], z.at[t, i], zf_s.at[i, k], z_r.at[i, t], sec(-2), k)
 
     def z_from(i, k):
-        rows = half_of(i)
-        return remote(zf.at[rows], z.at[k, rows], zf_s.at[i, k], z_r.at[i, k], sec(-2), k)
+        return remote(zf.at[i], z.at[k, i], zf_s.at[i, k], z_r.at[i, k], sec(-2), k)
 
     def g_copy(i, p):
         at = (chunk_of(i), cols(p))
         return remote(out.at[at], g.at[at], g_s.at[i, p], g_r.at[i, p], sec(-1), t)
 
-    def add_own(i, p, entering, pre_grad):
+    def add_own(i, p, entering):
         passed = entering.astype(F32) + own[:, cols(p)]
         out[chunk_of(i), cols(p)] = passed.astype(BF)
         g_copy(i, p).start()
 
     def pre_grad_of(i, from_above):
-        total = z[0, half_of(i)] + z[1, half_of(i)]
+        total = z[0, i].astype(F32) + z[1, i].astype(F32)
         if from_above:
-            total = total + q[half_of(i)]
-        pre_grad = (unpacked(total) * slope[chunk_of(i)]).astype(BF)
+            total = total + q[i].astype(F32)
+        return (unpacked(total) * slope[chunk_of(i)]).astype(BF)
+
+    def own_term(pre_grad):
         own[...] = dot(pre_grad, wu[...])
-        return pre_grad
 
     def send_q(i, pre_grad):
-        qsend[half_of(i)] = packed(dot(pre_grad, near[...]))
+        qsend[i] = packed(dot(pre_grad, near[...]))
         q_copy(i).start()
 
     def send_near(i):
-        zn[half_of(i)] = packed(dot_t(g[chunk_of(i)], wd1[...]))
+        zn[i] = packed(dot_t(g[chunk_of(i)], wd1[...]))
         for k in range(2):
             zn_copy(i, k).start()
 
     @pl.when(s == top)
     def _():
-        base_copy.wait()
-
         def first(i, _):
-            pre_grad = pre_grad_of(i, False)
+            own_term(pre_grad_of(i, False))
             for p in range(PIECES):
-                add_own(i, p, cot[chunk_of(i), cols(p)], pre_grad)
+                add_own(i, p, cot[chunk_of(i), cols(p)])
             return 0
 
-        lax.fori_loop(0, CHUNKS, first, 0)
+        for k in range(GROUPS):
+            base_from[k].wait_recv()
+            lax.fori_loop(k * GROUP // CHUNK, (k + 1) * GROUP // CHUNK, first, 0)
+        for k in range(GROUPS):
+            base_copy[k].wait_send()
         g[...] = cot[...]
 
     def own_base(i):
         for p in range(PIECES):
             g_copy(i, p).wait_recv()
         part_sum = packed(dot_t(g[chunk_of(i)], wd[...]))
-        za[half_of(i)] = part_sum
+        za[i] = part_sum
         za_copy(i).start()
-        z[t, half_of(i)] = part_sum
+        z[t, i] = part_sum
 
     def second(i):
-        remote(za.at[half_of(i)], z.at[other, half_of(i)], za_s.at[i], z_r.at[i, other], s, other).wait_recv()
+        remote(za.at[i], z.at[other, i], za_s.at[i], z_r.at[i, other], s, other).wait_recv()
         pre_grad = pre_grad_of(i, False)
+        own_term(pre_grad)
         for p in range(PIECES):
-            add_own(i, p, g[chunk_of(i), cols(p)], pre_grad)
+            add_own(i, p, g[chunk_of(i), cols(p)])
         return pre_grad
 
     @pl.when(s == top - 1)
@@ -245,8 +281,15 @@
         send_near(0)
         send_near(1)
 
-    dn.wait_recv()
-    m2s[...] = dot_t(wu1[...], wd1[...])
+    @pl.when(takes_dn)
+    def _():
+        dn.wait_recv()
+        m2s[...] = dot_t(wu1[...], wd1[...])
+
+    @pl.when(jnp.logical_not(takes_dn))
+    def _():
+        m2s[...] = jnp.zeros_like(m2s)
+
     m2_copy = [remote(m2s, m2.at[t], m2_s.at[k], m2_r.at[t], sec(1), k) for k in range(2)]
     m2_from = [remote(m2s, m2.at[k], m2_s.at[k], m2_r.at[k], sec(1), k) for k in range(2)]
     for copy in m2_copy:
@@ -254,7 +297,7 @@
 
     @pl.when(s == top - 1)
     def _():
-        qsend[half_of(0)] = packed(second(0).astype(F32))
+        kept[...] = second(0)
         own_base(2)
         send_near(2)
 
@@ -263,7 +306,7 @@
 
     @pl.when(s == top - 1)
     def _():
-        send_q(0, unpacked(qsend[half_of(0)]).astype(BF))
+        send_q(0, kept[...])
 
         def rest(i, _):
             send_q(i, second(i))
@@ -285,27 +328,26 @@
     sends_near = jnp.logical_or(s == top - 1, s == top - 2)
     sends_far = jnp.logical_and(s >= 3, s <= top - 2)
 
-    def relay(i, _):
+    def send_far(i, ahead):
+        zf[i] = packed(ahead)
+        for k in range(2):
+            zf_copy(i, k).start()
+
+    def arrive(i):
         z_from(i, 0).wait_recv()
         z_from(i, 1).wait_recv()
         q_copy(i).wait_recv()
-        pre_grad = pre_grad_of(i, True)
-
-        @pl.when(s >= 2)
-        def _():
+        return pre_grad_of(i, True)
+
+    @pl.when(s == top - 2)
+    def _():
+        def third(i, _):
+            pre_grad = arrive(i)
             send_q(i, pre_grad)
-
-        @pl.when(jnp.logical_and(s != top - 2, i == 0))
-        def _():
-            for p in range(PARTS):
-                up2[p].wait_recv()
-
-        for p in range(PIECES):
-            g_copy(i, p).wait_recv()
-            add_own(i, p, g[chunk_of(i), cols(p)], pre_grad)
-
-        @pl.when(s == top - 2)
-        def _():
+            own_term(pre_grad)
+            for p in range(PIECES):
+                g_copy(i, p).wait_recv()
+                add_own(i, p, g[chunk_of(i), cols(p)])
             send_near(i)
 
             @pl.when(i == 0)
@@ -313,17 +355,39 @@
                 for p in range(PARTS):
                     up2[p].wait_recv()
 
-        @pl.when(s >= 3)
-        def _():
-            ahead = dot(pre_grad, far[...]) + dot_t(g[chunk_of(i)], wd2[...])
-            zf[half_of(i)] = packed(ahead)
-            for k in range(2):
-                zf_copy(i, k).start()
-
-        return 0
-
-    @pl.when(jnp.logical_and(s >= 1, s <= top - 2))
-    def _():
+            send_far(i, dot(pre_grad, far[...]) + dot_t(g[chunk_of(i)], wd2[...]))
+            return 0
+
+        lax.fori_loop(0, CHUNKS, third, 0)
+
+    @pl.when(jnp.logical_and(s >= 1, s <= top - 3))
+    def _():
+        for p in range(PARTS):
+            up2[p].wait_recv()
+
+        def relay(i, _):
+            pre_grad = arrive(i)
+
+            @pl.when(s >= 2)
+            def _():
+                send_q(i, pre_grad)
+
+            own_term(pre_grad)
+            ahead = dot(pre_grad, far[...])
+            for p in range(PIECES):
+                g_copy(i, p).wait_recv()
+                entering = g[chunk_of(i), cols(p)]
+                if p < PIECES - 1:
+                    add_own(i, p, entering)
+                ahead = ahead + dot_t(entering, wd2[:, cols(p)])
+
+            @pl.when(s >= 3)
+            def _():
+                send_far(i, ahead)
+
+            add_own(i, PIECES - 1, entering)
+            return 0
+
         lax.fori_loop(0, CHUNKS, relay, 0)
 
     @pl.when(s == 0)
@@ -335,21 +399,8 @@
 
         lax.fori_loop(0, CHUNKS, last, 0)
 
-    u_of = lax.broadcasted_iota(jnp.int32, (LOW, SPAN), 0)
-    n_of = lax.broadcasted_iota(jnp.int32, (LOW, SPAN), 1)
-    row_basis = basis(freqs_along(freq_ref, 0, u_of), n_of)
-    u_t = lax.broadcasted_iota(jnp.int32, (SPAN, LOW), 1)
-    n_t = lax.broadcasted_iota(jnp.int32, (SPAN, LOW), 0)
-    row_basis_t = basis(freqs_along(freq_ref, 0, u_t), n_t)
-    at_row = lax.broadcasted_iota(jnp.int32, (2 * SPAN, 2 * SPAN), 0)
-    at_col = lax.broadcasted_iota(jnp.int32, (2 * SPAN, 2 * SPAN), 1)
-    pair_basis = jnp.where(
-        at_col // LOW == at_row // SPAN,
-        basis(freqs_along(freq_ref, 1, lax.rem(at_col, LOW)), lax.rem(at_row, SPAN)),
-        0.0,
-    )
-
     loads[4].wait()
+    row_basis, row_basis_t, pair_basis = row_ref[...], row_t_ref[...], pair_ref[...]
     grad = lax.dot_general(
         hidden[...], g[...], (((0,), (0,)), ((), ())), preferred_element_type=F32
     )
@@ -382,14 +433,16 @@
         [back[k * LOW : (k + 1) * LOW] for k in range(COLS // (2 * SPAN))], axis=1
     )
     decoded = dot(row_basis_t, wide, HIGH)
-    acc[...] = jnp.where(synced, acc[...] - decoded, acc[...])
-    store = pltpu.make_async_copy(acc, delta_hbm, load_sem.at[5])
-    store.start()
+    delta_ref[...] = jnp.where(synced, acc[...] - decoded, acc[...])
 
     for p in range(PARTS):
         up1[p].wait_send()
         up2[p].wait_send()
-    dn.wait_send()
+
+    @pl.when(sends_dn)
+    def _():
+        dn.wait_send()
+
     m1_copy.wait_send()
     for copy in m2_copy:
         copy.wait_send()
@@ -438,7 +491,6 @@
     back = dot_t(mean, pair_basis, HIGH)
     wide = jnp.concatenate([back[k * LOW : (k + 1) * LOW] for k in range(SHARE // LOW)], axis=1)
     change_ref[...] = dot(row_basis_t, wide, HIGH)
-    store.wait()
     for d in range(1, REPLICAS):
         c_copy(d).wait_send()
 
@@ -447,20 +499,23 @@
     cotangent, saved_pre, up_band, down_band, accumulated, outer_momentum, band_freqs, sync_flags
 ):
     vmem = pl.BlockSpec(memory_space=pltpu.VMEM)
-    smem = pl.BlockSpec(memory_space=pltpu.SMEM)
-    hbm = pl.BlockSpec(memory_space=pl.ANY)
+    hbm = pl.BlockSpec(memory_space=pltpu.HBM)
     share = COLS // REPLICAS
     dma = pltpu.SemaphoreType.DMA
-    half_rows = ROWS // 2
     delta, change = pl.pallas_call(
         kernel,
         out_shape=(
             jax.ShapeDtypeStruct((BAND, COLS), F32),
             jax.ShapeDtypeStruct((BAND, share), F32),
         ),
-        in_specs=[smem, smem, hbm, hbm, hbm, hbm, hbm],
-        out_specs=(hbm, vmem),
+        in_specs=[hbm] * 7,
+        out_specs=(vmem, vmem),
         scratch_shapes=[
+            pltpu.SMEM((2, LOW), jnp.int32),
+            pltpu.SMEM((1,), jnp.int32),
+            pltpu.VMEM((LOW, SPAN), F32),
+            pltpu.VMEM((SPAN, LOW), F32),
+            pltpu.VMEM((2 * SPAN, 2 * SPAN), F32),
             pltpu.VMEM((ROWS, COLS), BF),
             pltpu.VMEM((ROWS, BAND), BF),
             pltpu.VMEM((BAND, COLS), BF),
@@ -471,12 +526,12 @@
             pltpu.VMEM((BAND, COLS), BF),
             pltpu.VMEM((BAND, COLS), BF),
             pltpu.VMEM((BAND, COLS), BF),
-            pltpu.VMEM((2, half_rows, 2 * BAND), F32),
-            pltpu.VMEM((half_rows, 2 * BAND), F32),
-            pltpu.VMEM((half_rows, 2 * BAND), F32),
-            pltpu.VMEM((half_rows, 2 * BAND), F32),
-            pltpu.VMEM((half_rows, 2 * BAND), F32),
-            pltpu.VMEM((half_rows, 2 * BAND), F32),
+            pltpu.VMEM((2, CHUNKS, HALF, 2 * BAND), BF),
+            pltpu.VMEM((CHUNKS, HALF, 2 * BAND), BF),
+            pltpu.VMEM((CHUNKS, HALF, 2 * BAND), BF),
+            pltpu.VMEM((CHUNKS, HALF, 2 * BAND), BF),
+            pltpu.VMEM((CHUNKS, HALF, 2 * BAND), BF),
+            pltpu.VMEM((CHUNKS, HALF, 2 * BAND), BF),
             pltpu.VMEM((2, BAND, BAND), F32),
             pltpu.VMEM((2, BAND, BAND), F32),
             pltpu.VMEM((BAND, BAND), F32),
@@ -486,20 +541,21 @@
             pltpu.VMEM((ROWS, BAND), F32),
             pltpu.VMEM((ROWS, BAND), BF),
             pltpu.VMEM((CHUNK, COLS), F32),
+            pltpu.VMEM((CHUNK, BAND), BF),
             pltpu.VMEM((REPLICAS * SHARE, 2 * SPAN), F32),
             pltpu.VMEM((REPLICAS, SHARE, 2 * SPAN), F32),
-            dma((6,)),
+            dma((7,)),
             dma((PARTS,)), dma((PARTS,)), dma((PARTS,)), dma((PARTS,)),
             dma, dma, dma, dma,
             dma((2,)), dma((2,)),
-            dma, dma,
+            dma((GROUPS,)), dma((GROUPS,)),
             dma((CHUNKS,)), dma((CHUNKS, 2)), dma((CHUNKS, 2)), dma((CHUNKS, 2)),
             dma((CHUNKS,)), dma((CHUNKS,)),
             dma((CHUNKS, PIECES)), dma((CHUNKS, PIECES)),
             dma((REPLICAS,)), dma((REPLICAS,)),
         ],
         compiler_params=pltpu.CompilerParams(
-            collective_id=0, has_side_effects=True, vmem_limit_bytes=60 << 20
+            collective_id=0, has_side_effects=True, vmem_limit_bytes=LIMIT << 20
         ),
         name="relay",
     )(

time: 141 us -> 138 us (0.979)
  Pallas kernels: 137 us -> 133 us
    pallas_call x1, Pallas kernels: 137 us -> 133 us  [local(): pl.pallas_call(kernel, out_shape=(jax.ShapeDtypeStruct((BAND, COLS), F32)...]
where the time goes in v3:
time: 138 us; the launch traced here: 137 us
  Pallas kernels  133 us (96%)
  other arithmetic  3.01 us (2%)
    pallas_call x1, Pallas kernels, local(): pl.pallas_call(kernel, out_shape=(jax.ShapeDtypeStruct((BAND, COLS), F32)...  133 us

profile of v3, /device:TPU:1, one launch (start us, length us, event | category | flops | bytes accessed | tf_op | source)
XLA Modules:
  0.0 137.4 jit_solution(9735850683135784990)
XLA Ops:
  1.3 0.0 copy-start
  1.3 133.0 %relay.1 = (f32[64,4096]{1,0:T(8,128)}, f32[64,256]{1,0:T(8,128)}) custom-call(s32[2,8]{1,0:T(2,128)} %freq_hbm.1, s32[1]{0:T(128)S(6)} %copy.11.flag_hbm, bf16[192,4096]{1,0:T(8,128)(2,1)} %bitcast.24, bf16[192,64]{1,0:T(8,128)(2,1)} %bitcast.27, bf16[64,4096]{1,0:T(8,128)(2,1)} %bitcast.25, bf16[64,4096]{1,0:T(8,128)(2,1)} %bitcast.26, f32[64,4096]{1,0:T(8,128)} %bitcast.23), custom_call_target="tpu_custom_call" | custom-call | tf_op jit(solution)/shard_map/relay/pallas_call | solution.py:505
  134.3 0.0 copy-done
  134.4 0.0 copy-start.1
  134.4 0.0 copy-start.2
  134.4 2.3 %bitcast_add_fusion = f32[1,64,4096]{2,1,0:T(8,128)} fusion(f32[1,64,4096]{2,1,0:T(8,128)S(1)} %copy-done, f32[64,4096]{1,0:T(8,128)} %get-tuple-element.5), kind=kLoop, calls=%fused_computation | loop fusion | flops 262144 | bytes 3145728 | tf_op jit(solution)/shard_map/add | solution.py:570
  136.7 0.0 copy-done.1
  136.7 0.0 copy-done.2
  136.7 0.7 select_bitcast_fusion
Async XLA Ops:
  1.3 133.1 %copy-start = (f32[1,64,4096]{2,1,0:T(8,128)S(1)}, f32[1,64,4096]{2,1,0:T(8,128)}, u32[]{:S(2)}) copy-start(f32[1,64,4096]{2,1,0:T(8,128)} %param.12) | copy-start | bytes 3145732
  134.4 2.4 %copy-start.1 = (f32[1,1,64,256]{3,2,1,0:T(8,128)S(1)}, f32[1,1,64,256]{3,2,1,0:T(8,128)}, u32[]{:S(2)}) copy-start(f32[1,1,64,256]{3,2,1,0:T(8,128)} %param.13) | copy-start | bytes 196612
  134.4 2.4 %copy-start.2 = (f32[64,256]{1,0:T(8,128)S(1)}, f32[64,256]{1,0:T(8,128)}, u32[]{:S(2)}) copy-start(f32[64,256]{1,0:T(8,128)} %get-tuple-element.6) | copy-start | bytes 196612

commit v4 on v3

--- a/solution.py
+++ b/solution.py
@@ -228,10 +228,13 @@
         qsend[i] = packed(dot(pre_grad, near[...]))
         q_copy(i).start()
 
-    def send_near(i):
-        zn[i] = packed(dot_t(g[chunk_of(i)], wd1[...]))
+    def send_near_sum(i, near_sum):
+        zn[i] = packed(near_sum)
         for k in range(2):
             zn_copy(i, k).start()
+
+    def send_near(i):
+        send_near_sum(i, dot_t(g[chunk_of(i)], wd1[...]))
 
     @pl.when(s == top)
     def _():
@@ -249,9 +252,11 @@
         g[...] = cot[...]
 
     def own_base(i):
+        base = jnp.zeros((CHUNK, BAND), F32)
         for p in range(PIECES):
             g_copy(i, p).wait_recv()
-        part_sum = packed(dot_t(g[chunk_of(i)], wd[...]))
+            base = base + dot_t(g[chunk_of(i), cols(p)], wd[:, cols(p)])
+        part_sum = packed(base)
         za[i] = part_sum
         za_copy(i).start()
         z[t, i] = part_sum
@@ -269,10 +274,12 @@
         own_base(0)
         own_base(1)
 
+    coupling = jnp.zeros((BAND, BAND), F32)
     for p in range(PARTS):
         up1[p].wait_recv()
         up2[p].start()
-    m1s[...] = dot_t(wu[...], wd1[...])
+        coupling = coupling + dot_t(wu[:, part(p)], wd1[:, part(p)])
+    m1s[...] = coupling.astype(BF)
     m1_copy = remote(m1s, m1.at[t], m1_s, m1_r, s, other)
     m1_copy.start()
 
@@ -284,7 +291,7 @@
     @pl.when(takes_dn)
     def _():
         dn.wait_recv()
-        m2s[...] = dot_t(wu1[...], wd1[...])
+        m2s[...] = dot_t(wu1[...], wd1[...]).astype(BF)
 
     @pl.when(jnp.logical_not(takes_dn))
     def _():
@@ -302,7 +309,7 @@
         send_near(2)
 
     m1_copy.wait_recv()
-    near[...] = (m1s[...] + m1[other]).astype(BF)
+    near[...] = (m1s[...].astype(F32) + m1[other].astype(F32)).astype(BF)
 
     @pl.when(s == top - 1)
     def _():
@@ -322,7 +329,7 @@
 
     for copy in m2_from:
         copy.wait_recv()
-    far[...] = (0.5 * (m2[0] + m2[1])).astype(BF)
+    far[...] = (0.5 * (m2[0].astype(F32) + m2[1].astype(F32))).astype(BF)
 
     sends_q = jnp.logical_and(s >= 2, s <= top - 1)
     sends_near = jnp.logical_or(s == top - 1, s == top - 2)
@@ -345,10 +352,15 @@
             pre_grad = arrive(i)
             send_q(i, pre_grad)
             own_term(pre_grad)
+            near_sum = jnp.zeros((CHUNK, BAND), F32)
             for p in range(PIECES):
                 g_copy(i, p).wait_recv()
-                add_own(i, p, g[chunk_of(i), cols(p)])
-            send_near(i)
+                entering = g[chunk_of(i), cols(p)]
+                if p < PIECES - 1:
+                    add_own(i, p, entering)
+                near_sum = near_sum + dot_t(entering, wd1[:, cols(p)])
+            send_near_sum(i, near_sum)
+            add_own(i, PIECES - 1, entering)
 
             @pl.when(i == 0)
             def _():
@@ -532,10 +544,10 @@
             pltpu.VMEM((CHUNKS, HALF, 2 * BAND), BF),
             pltpu.VMEM((CHUNKS, HALF, 2 * BAND), BF),
             pltpu.VMEM((CHUNKS, HALF, 2 * BAND), BF),
-            pltpu.VMEM((2, BAND, BAND), F32),
-            pltpu.VMEM((2, BAND, BAND), F32),
-            pltpu.VMEM((BAND, BAND), F32),
-            pltpu.VMEM((BAND, BAND), F32),
+            pltpu.VMEM((2, BAND, BAND), BF),
+            pltpu.VMEM((2, BAND, BAND), BF),
+            pltpu.VMEM((BAND, BAND), BF),
+            pltpu.VMEM((BAND, BAND), BF),
             pltpu.VMEM((BAND, BAND), BF),
             pltpu.VMEM((BAND, BAND), BF),
             pltpu.VMEM((ROWS, BAND), F32),

time: 138 us -> 136 us (0.986)
  Pallas kernels: 133 us -> 131 us
    pallas_call x1, Pallas kernels: 133 us -> 131 us  [local(): pl.pallas_call(kernel, out_shape=(jax.ShapeDtypeStruct((BAND, COLS), F32)...]
where the time goes in v4:
time: 136 us
  Pallas kernels  131 us (96%)
  other arithmetic  3.01 us (2%)
    pallas_call x1, Pallas kernels, local(): pl.pallas_call(kernel, out_shape=(jax.ShapeDtypeStruct((BAND, COLS), F32)...  131 us

profile of v4, /device:TPU:1, one launch (start us, length us, event | category | flops | bytes accessed | tf_op | source)
XLA Modules:
  0.0 135.8 jit_solution(12743631004859903370)
XLA Ops:
  1.3 0.0 copy-start
  1.3 131.5 %relay.1 = (f32[64,4096]{1,0:T(8,128)}, f32[64,256]{1,0:T(8,128)}) custom-call(s32[2,8]{1,0:T(2,128)} %freq_hbm.1, s32[1]{0:T(128)S(6)} %copy.11.flag_hbm, bf16[192,4096]{1,0:T(8,128)(2,1)} %bitcast.24, bf16[192,64]{1,0:T(8,128)(2,1)} %bitcast.27, bf16[64,4096]{1,0:T(8,128)(2,1)} %bitcast.25, bf16[64,4096]{1,0:T(8,128)(2,1)} %bitcast.26, f32[64,4096]{1,0:T(8,128)} %bitcast.23), custom_call_target="tpu_custom_call" | custom-call | tf_op jit(solution)/shard_map/relay/pallas_call | solution.py:517
  132.8 0.0 copy-done
  132.8 0.0 copy-start.1
  132.8 0.0 copy-start.2
  132.8 2.3 %bitcast_add_fusion = f32[1,64,4096]{2,1,0:T(8,128)} fusion(f32[1,64,4096]{2,1,0:T(8,128)S(1)} %copy-done, f32[64,4096]{1,0:T(8,128)} %get-tuple-element.5), kind=kLoop, calls=%fused_computation | loop fusion | flops 262144 | bytes 3145728 | tf_op jit(solution)/shard_map/add | solution.py:582
  135.2 0.0 copy-done.1
  135.2 0.0 copy-done.2
  135.2 0.7 select_bitcast_fusion
Async XLA Ops:
  1.3 131.5 %copy-start = (f32[1,64,4096]{2,1,0:T(8,128)S(1)}, f32[1,64,4096]{2,1,0:T(8,128)}, u32[]{:S(2)}) copy-start(f32[1,64,4096]{2,1,0:T(8,128)} %param.12) | copy-start | bytes 3145732
  132.8 2.4 %copy-start.1 = (f32[1,1,64,256]{3,2,1,0:T(8,128)S(1)}, f32[1,1,64,256]{3,2,1,0:T(8,128)}, u32[]{:S(2)}) copy-start(f32[1,1,64,256]{3,2,1,0:T(8,128)} %param.13) | copy-start | bytes 196612
  132.8 2.4 %copy-start.2 = (f32[64,256]{1,0:T(8,128)S(1)}, f32[64,256]{1,0:T(8,128)}, u32[]{:S(2)}) copy-start(f32[64,256]{1,0:T(8,128)} %get-tuple-element.6) | copy-start | bytes 196612

commit v5 on v4

--- a/solution.py
+++ b/solution.py
@@ -102,9 +102,6 @@
             )
         )
     ]
-    for load in loads:
-        load.start()
-
     barrier = pltpu.get_barrier_semaphore()
     for offset in (-2, -1, 1, 2):
         for tensor in range(2):
@@ -116,6 +113,8 @@
         pl.semaphore_signal(
             barrier, inc=1, device_id=(lax.rem(r + d, REPLICAS), s, t), device_id_type=MESH
         )
+    for load in loads:
+        load.start()
     pl.semaphore_wait(barrier, 9 + REPLICAS - 1)
 
     def part(p):
@@ -230,7 +229,7 @@
 
     def send_near_sum(i, near_sum):
         zn[i] = packed(near_sum)
-        for k in range(2):
+        for k in (other, t):
             zn_copy(i, k).start()
 
     def send_near(i):
@@ -337,7 +336,7 @@
 
     def send_far(i, ahead):
         zf[i] = packed(ahead)
-        for k in range(2):
+        for k in (other, t):
             zf_copy(i, k).start()
 
     def arrive(i):

time: 136 us -> 136 us (level)
  no operation moved by 1% of the time
where the time goes in v5:
time: 136 us
  Pallas kernels  131 us (96%)
  other arithmetic  3.01 us (2%)
    pallas_call x1, Pallas kernels, local(): pl.pallas_call(kernel, out_shape=(jax.ShapeDtypeStruct((BAND, COLS), F32)...  131 us

profile of v5, /device:TPU:1, one launch (start us, length us, event | category | flops | bytes accessed | tf_op | source)
XLA Modules:
  0.0 135.8 jit_solution(14554716078224410714)
XLA Ops:
  1.3 0.0 copy-start
  1.3 131.4 %relay.1 = (f32[64,4096]{1,0:T(8,128)}, f32[64,256]{1,0:T(8,128)}) custom-call(s32[2,8]{1,0:T(2,128)} %freq_hbm.1, s32[1]{0:T(128)S(6)} %copy.11.flag_hbm, bf16[192,4096]{1,0:T(8,128)(2,1)} %bitcast.24, bf16[192,64]{1,0:T(8,128)(2,1)} %bitcast.27, bf16[64,4096]{1,0:T(8,128)(2,1)} %bitcast.25, bf16[64,4096]{1,0:T(8,128)(2,1)} %bitcast.26, f32[64,4096]{1,0:T(8,128)} %bitcast.23), custom_call_target="tpu_custom_call" | custom-call | tf_op jit(solution)/shard_map/relay/pallas_call | solution.py:516
  132.7 0.0 copy-done
  132.7 0.0 copy-start.1
  132.7 0.0 copy-start.2
  132.8 2.3 %bitcast_add_fusion = f32[1,64,4096]{2,1,0:T(8,128)} fusion(f32[1,64,4096]{2,1,0:T(8,128)S(1)} %copy-done, f32[64,4096]{1,0:T(8,128)} %get-tuple-element.5), kind=kLoop, calls=%fused_computation | loop fusion | flops 262144 | bytes 3145728 | tf_op jit(solution)/shard_map/add | solution.py:581
  135.1 0.0 copy-done.1
  135.1 0.0 copy-done.2
  135.1 0.7 select_bitcast_fusion
Async XLA Ops:
  1.3 131.4 %copy-start = (f32[1,64,4096]{2,1,0:T(8,128)S(1)}, f32[1,64,4096]{2,1,0:T(8,128)}, u32[]{:S(2)}) copy-start(f32[1,64,4096]{2,1,0:T(8,128)} %param.12) | copy-start | bytes 3145732
  132.7 2.4 %copy-start.1 = (f32[1,1,64,256]{3,2,1,0:T(8,128)S(1)}, f32[1,1,64,256]{3,2,1,0:T(8,128)}, u32[]{:S(2)}) copy-start(f32[1,1,64,256]{3,2,1,0:T(8,128)} %param.13) | copy-start | bytes 196612
  132.7 2.4 %copy-start.2 = (f32[64,256]{1,0:T(8,128)S(1)}, f32[64,256]{1,0:T(8,128)}, u32[]{:S(2)}) copy-start(f32[64,256]{1,0:T(8,128)} %get-tuple-element.6) | copy-start | bytes 196612
